TPU v7x, 32 devices: a whole 2x2x4 slice. The times are simulated.
32 devices in a mesh: section: 2 (over y), dp: 16 (over z, x, core).
Axes of the slice: x: 2, y: 2, z: 4, core: 2. Of those that a mesh axis runs over, the one named last changes fastest.
Arguments:
- layer_input: bfloat16 [2, 2, 16, 1024, 512], P('section', None, 'dp'), may hold values from -6 to 6
- cotangent: bfloat16 [2, 16, 1024, 512], P(None, 'dp'), may hold values from -6 to 6
- src_segments: int32 [2, 16, 1024], P(None, 'dp'), may hold values from 0 to 3, as said below
- tgt_segments: int32 [2, 16, 1024], P(None, 'dp'), may hold values from 0 to 3, as said below
- attn_qkv: bfloat16 [2, 512, 1536], P('section'), may hold values from -0.25 to 0.25
- attn_out: bfloat16 [2, 512, 512], P('section'), may hold values from -1 to 1
- cross_proj: bfloat16 [2, 512, 1024], P('section'), may hold values from -0.5 to 0.5
- ffn_in: bfloat16 [2, 512, 2048], P('section'), may hold values from -0.25 to 0.25
- ffn_in_bias: float32 [2, 2048], P('section'), may hold values from -3 to 3
- ffn_out: bfloat16 [2, 2048, 512], P('section'), may hold values from -0.125 to 0.125
- ffn_out_bias: float32 [2, 512], P('section'), may hold values from -3 to 3
- norm_gain: float32 [2, 3, 512], P('section'), may hold values from 0.1 to 1.9
- norm_bias: float32 [2, 3, 512], P('section'), may hold values from -3 to 3
Outputs:
- layer_output: bfloat16 [2, 2, 16, 1024, 512], P('section', None, 'dp')
- input_grad: float32 [2, 2, 16, 1024, 512], P('section', None, 'dp')
- attn_qkv_grad: float32 [2, 512, 1536], P('section')
- attn_out_grad: float32 [2, 512, 512], P('section')
- cross_proj_grad: float32 [2, 512, 1024], P('section')
- ffn_in_grad: float32 [2, 512, 2048], P('section')
- ffn_in_bias_grad: float32 [2, 2048], P('section')
- ffn_out_grad: float32 [2, 2048, 512], P('section')
- ffn_out_bias_grad: float32 [2, 512], P('section')
- norm_gain_grad: float32 [2, 3, 512], P('section')
- norm_bias_grad: float32 [2, 3, 512], P('section')
Inputs may be any that keep to these rules, and one draw needn't show every extreme that they name: `src_segments`: in every packed row the document numbers never fall and take every value of 0 to 3, each on 128 tokens or more. `tgt_segments`: in every packed row the document numbers never fall and take every value of 0 to 3, each on 128 tokens or more.
All inputs are finite; a program needn't handle non-finite values.
Results may differ from a plain program's by a relative error of at most 0.04.
Values may be sent and summed in bfloat16 or wider, within the bound.
A program may use at most 320 MiB of HBM per device.

v0:
```python
import functools
import math

import jax
import jax.numpy as jnp
from jax import lax
from jax.sharding import PartitionSpec as P

HEADS = 8


EPSILON = 1e-05
NEGATIVE = -1000000000.0


def swapped(value, axis, bit):
    mask = 2**bit
    pairs = [(source, source ^ mask) for source in range(lax.axis_size(axis))]
    return lax.ppermute(value, axis, pairs)


def product(left, right):
    return jnp.dot(left, right, preferred_element_type=jnp.float32)


def inner_rows(left, right):
    return lax.dot_general(
        left, right, (((0,), (0,)), ((), ())), preferred_element_type=jnp.float32
    )


def times_transposed(left, right):
    return lax.dot_general(
        left, right, (((1,), (1,)), ((), ())), preferred_element_type=jnp.float32
    )


def norm_rows(value, gain, shift):
    centered = value - jnp.mean(value, axis=-1, keepdims=True)
    spread = jnp.mean(centered * centered, axis=-1, keepdims=True)
    return centered * lax.rsqrt(spread + EPSILON) * gain + shift


def gelu_exact(value):
    return jax.nn.gelu(value, approximate=False)


def block_scores(scaled_query, key_heads, block_ids, key_ids, block_index, block, causal):
    scores = jnp.einsum("qhd,khd->hqk", scaled_query, key_heads, preferred_element_type=jnp.float32)
    allowed = block_ids[:, None] == key_ids[None, :]
    if causal:
        query_pos = block_index * block + jnp.arange(block, dtype=jnp.int32)
        key_pos = jnp.arange(key_ids.shape[0], dtype=jnp.int32)
        allowed = allowed & (query_pos[:, None] >= key_pos[None, :])
    return jnp.where(allowed[None], scores, NEGATIVE)


def attend_rows(query, keys, values, query_ids, key_ids, causal):
    rows, length, width = query.shape
    span = keys.shape[1]
    head_dim = width // HEADS
    scale = 1.0 / math.sqrt(head_dim)
    block = min(512, length)
    blocks = length // block

    def one_row(item):
        row_query, row_keys, row_values, row_qids, row_kids = item
        key_heads = row_keys.reshape(span, HEADS, head_dim)
        value_heads = row_values.reshape(span, HEADS, head_dim)

        def one_block(block_query, block_ids, block_index, limit):
            scaled_query = block_query * scale
            scores = block_scores(
                scaled_query,
                key_heads[:limit],
                block_ids,
                row_kids[:limit],
                block_index,
                block,
                causal,
            )
            highest = jnp.max(scores, axis=-1, keepdims=True)
            raised = jnp.exp(scores - highest)
            totals = jnp.sum(raised, axis=-1, keepdims=True)
            weights = (raised / totals).astype(jnp.bfloat16)
            mixed = jnp.einsum(
                "hqk,khd->qhd", weights, value_heads[:limit], preferred_element_type=jnp.float32
            )
            return (
                mixed.reshape(block, width).astype(jnp.bfloat16),
                (highest + jnp.log(totals))[..., 0],
            )

        query_blocks = row_query.reshape(blocks, block, HEADS, head_dim)
        id_blocks = row_qids.reshape(blocks, block)
        if causal:
            results = [
                one_block(query_blocks[index], id_blocks[index], index, (index + 1) * block)
                for index in range(blocks)
            ]
            mixed = jnp.stack([item_pair[0] for item_pair in results])
            logsum = jnp.stack([item_pair[1] for item_pair in results])
        else:
            pieces = (query_blocks, id_blocks, jnp.arange(blocks, dtype=jnp.int32))
            mixed, logsum = lax.map(
                lambda piece: one_block(piece[0], piece[1], piece[2], span), pieces
            )
        return (mixed.reshape(length, width), logsum)

    return lax.map(one_row, (query, keys, values, query_ids, key_ids))


def attend_back(query, keys, values, out_grad, logsum, query_ids, key_ids, causal):
    rows, length, width = query.shape
    span = keys.shape[1]
    head_dim = width // HEADS
    scale = 1.0 / math.sqrt(head_dim)
    block = min(512, length)
    blocks = length // block

    def one_row(item):
        row_query, row_keys, row_values, row_grad, row_logsum, row_qids, row_kids = item
        key_heads = row_keys.reshape(span, HEADS, head_dim)
        value_heads = row_values.reshape(span, HEADS, head_dim)

        def one_block(block_query, block_grad, block_logsum, block_ids, block_index, limit):
            scaled_query = block_query * scale
            near_keys = key_heads[:limit]
            near_values = value_heads[:limit]
            scores = block_scores(
                scaled_query, near_keys, block_ids, row_kids[:limit], block_index, block, causal
            )
            chances = jnp.exp(scores - block_logsum[..., None])
            weights = chances.astype(jnp.bfloat16)
            chance_grad = jnp.einsum(
                "qhd,khd->hqk", block_grad, near_values, preferred_element_type=jnp.float32
            )
            centre = jnp.sum(chances * chance_grad, axis=-1, keepdims=True)
            score_grad = (chances * (chance_grad - centre)).astype(jnp.bfloat16)
            query_grad = (
                jnp.einsum(
                    "hqk,khd->qhd", score_grad, near_keys, preferred_element_type=jnp.float32
                )
                * scale
            )
            key_part = jnp.einsum(
                "hqk,qhd->khd", score_grad, scaled_query, preferred_element_type=jnp.float32
            )
            value_part = jnp.einsum(
                "hqk,qhd->khd", weights, block_grad, preferred_element_type=jnp.float32
            )
            return (key_part, value_part, query_grad.reshape(block, width))

        start = jnp.zeros((span, HEADS, head_dim), jnp.float32)
        query_blocks = row_query.reshape(blocks, block, HEADS, head_dim)
        grad_blocks = row_grad.reshape(blocks, block, HEADS, head_dim)
        id_blocks = row_qids.reshape(blocks, block)
        if causal:
            key_grad = start
            value_grad = start
            query_parts = []
            for index in range(blocks):
                limit = (index + 1) * block
                key_part, value_part, query_part = one_block(
                    query_blocks[index],
                    grad_blocks[index],
                    row_logsum[index],
                    id_blocks[index],
                    index,
                    limit,
                )
                key_grad = key_grad.at[:limit].add(key_part)
                value_grad = value_grad.at[:limit].add(value_part)
                query_parts.append(query_part)
            query_grad = jnp.stack(query_parts)
        else:

            def scan_block(carry, piece):
                key_part, value_part, query_part = one_block(
                    piece[0], piece[1], piece[2], piece[3], piece[4], span
                )
                return ((carry[0] + key_part, carry[1] + value_part), query_part)

            pieces = (
                query_blocks,
                grad_blocks,
                row_logsum,
                id_blocks,
                jnp.arange(blocks, dtype=jnp.int32),
            )
            (key_grad, value_grad), query_grad = lax.scan(scan_block, (start, start), pieces)
        return (
            query_grad.reshape(length, width),
            key_grad.reshape(span, width),
            value_grad.reshape(span, width),
        )

    return lax.map(one_row, (query, keys, values, out_grad, logsum, query_ids, key_ids))


def self_forward(flat, doc_ids, causal, w_joint, w_out, gain, shift):
    rows, length = doc_ids.shape
    width = flat.shape[1]
    joint = product(flat, w_joint).astype(jnp.bfloat16).reshape(rows, length, 3 * width)
    attended, logsum = attend_rows(
        joint[..., :width],
        joint[..., width : 2 * width],
        joint[..., 2 * width :],
        doc_ids,
        doc_ids,
        causal,
    )
    attended_flat = attended.reshape(rows * length, width)
    residual = flat.astype(jnp.float32) + product(attended_flat, w_out)
    hidden, back_norm = jax.vjp(norm_rows, residual, gain, shift)
    return (hidden, (joint, attended_flat, logsum, back_norm))


def self_backward(hidden_grad, flat, doc_ids, causal, w_joint, w_out, saved):
    joint, attended_flat, logsum, back_norm = saved
    rows, length = doc_ids.shape
    width = flat.shape[1]
    residual_grad, gain_grad, shift_grad = back_norm(hidden_grad)
    branch_low = residual_grad.astype(jnp.bfloat16)
    out_weight_grad = inner_rows(attended_flat, branch_low)
    attended_grad = (
        times_transposed(branch_low, w_out).astype(jnp.bfloat16).reshape(rows, length, width)
    )
    query_grad, key_grad, value_grad = attend_back(
        joint[..., :width],
        joint[..., width : 2 * width],
        joint[..., 2 * width :],
        attended_grad,
        logsum,
        doc_ids,
        doc_ids,
        causal,
    )
    joint_grad = (
        jnp.concatenate([query_grad, key_grad, value_grad], axis=-1)
        .astype(jnp.bfloat16)
        .reshape(rows * length, 3 * width)
    )
    joint_weight_grad = inner_rows(flat, joint_grad)
    token_grad = residual_grad + times_transposed(joint_grad, w_joint)
    return (token_grad, joint_weight_grad, out_weight_grad, gain_grad, shift_grad)


def feed_forward(hidden, w_in, b_in, w_back, b_back):
    hidden_low = hidden.astype(jnp.bfloat16)
    pre_act = product(hidden_low, w_in) + b_in
    activation, back_act = jax.vjp(gelu_exact, pre_act)
    activation_low = activation.astype(jnp.bfloat16)
    return (product(activation_low, w_back) + b_back, (hidden_low, activation_low, back_act))


def feed_backward(value_grad, w_in, w_back, saved):
    hidden_low, activation_low, back_act = saved
    value_low = value_grad.astype(jnp.bfloat16)
    back_weight_grad = inner_rows(activation_low, value_low)
    back_bias_grad = jnp.sum(value_low.astype(jnp.float32), axis=0)
    (pre_grad,) = back_act(times_transposed(value_low, w_back))
    pre_low = pre_grad.astype(jnp.bfloat16)
    in_weight_grad = inner_rows(hidden_low, pre_low)
    in_bias_grad = jnp.sum(pre_low.astype(jnp.float32), axis=0)
    return (
        times_transposed(pre_low, w_in),
        in_weight_grad,
        in_bias_grad,
        back_weight_grad,
        back_bias_grad,
    )


def encoder_forward(tokens, source_ids, params):
    w_joint, w_out, w_cross, w_in, b_in, w_back, b_back, gains, shifts = params
    width = tokens.shape[-1]
    flat = tokens.reshape(-1, width)
    hidden_one, self_saved = self_forward(
        flat, source_ids, False, w_joint, w_out, gains[0], shifts[0]
    )
    feed_value, feed_saved = feed_forward(hidden_one, w_in, b_in, w_back, b_back)
    hidden_two, back_two = jax.vjp(norm_rows, hidden_one + feed_value, gains[1], shifts[1])
    memory, back_three = jax.vjp(norm_rows, hidden_two, gains[2], shifts[2])
    return (memory.astype(jnp.bfloat16), (flat, self_saved, feed_saved, back_two, back_three))


def encoder_backward(source_ids, params, memory_low, saved, keys_grad):
    w_joint, w_out, w_cross, w_in, b_in, w_back, b_back, gains, shifts = params
    flat, self_saved, feed_saved, back_two, back_three = saved
    memory_grad = times_transposed(keys_grad, w_cross)
    cross_weight_grad = inner_rows(memory_low, keys_grad)
    two_grad, gain_three, shift_three = back_three(memory_grad)
    residual_grad, gain_two, shift_two = back_two(two_grad)
    hidden_extra, in_weight, in_bias, back_weight, back_bias = feed_backward(
        residual_grad, w_in, w_back, feed_saved
    )
    token_grad, joint_weight, out_weight, gain_one, shift_one = self_backward(
        residual_grad + hidden_extra, flat, source_ids, False, w_joint, w_out, self_saved
    )
    grads = (
        joint_weight,
        out_weight,
        cross_weight_grad,
        in_weight,
        in_bias,
        back_weight,
        back_bias,
        jnp.stack([gain_one, gain_two, gain_three]),
        jnp.stack([shift_one, shift_two, shift_three]),
    )
    return (token_grad, grads)


def decoder_pass(tokens, target_ids, source_ids, cross_keys, cotangent, params):
    w_joint, w_out, w_cross, w_in, b_in, w_back, b_back, gains, shifts = params
    rows, length, width = tokens.shape
    flat = tokens.reshape(-1, width)
    hidden_one, self_saved = self_forward(
        flat, target_ids, True, w_joint, w_out, gains[0], shifts[0]
    )
    hidden_low = hidden_one.astype(jnp.bfloat16)
    cross_query = (
        product(hidden_low, w_cross[:, :width]).astype(jnp.bfloat16).reshape(rows, length, width)
    )
    cross_key_part = cross_keys[..., :width]
    cross_value_part = cross_keys[..., width:]
    crossed, cross_logsum = attend_rows(
        cross_query, cross_key_part, cross_value_part, target_ids, source_ids, False
    )
    crossed_flat = crossed.reshape(rows * length, width)
    hidden_two, back_two = jax.vjp(
        norm_rows, hidden_one + product(crossed_flat, w_cross[:, width:]), gains[1], shifts[1]
    )
    feed_value, feed_saved = feed_forward(hidden_two, w_in, b_in, w_back, b_back)
    output, back_three = jax.vjp(norm_rows, hidden_two + feed_value, gains[2], shifts[2])
    residual_three, gain_three, shift_three = back_three(
        cotangent.reshape(-1, width).astype(jnp.float32)
    )
    hidden_extra, in_weight, in_bias, back_weight, back_bias = feed_backward(
        residual_three, w_in, w_back, feed_saved
    )
    residual_two, gain_two, shift_two = back_two(residual_three + hidden_extra)
    cross_low = residual_two.astype(jnp.bfloat16)
    cross_out_weight = inner_rows(crossed_flat, cross_low)
    crossed_grad = (
        times_transposed(cross_low, w_cross[:, width:])
        .astype(jnp.bfloat16)
        .reshape(rows, length, width)
    )
    query_grad, key_grad, value_grad = attend_back(
        cross_query,
        cross_key_part,
        cross_value_part,
        crossed_grad,
        cross_logsum,
        target_ids,
        source_ids,
        False,
    )
    query_low = query_grad.reshape(-1, width).astype(jnp.bfloat16)
    keys_grad = jnp.concatenate([key_grad, value_grad], axis=-1).astype(jnp.bfloat16)
    cross_query_weight = inner_rows(hidden_low, query_low)
    hidden_grad = residual_two + times_transposed(query_low, w_cross[:, :width])
    token_grad, joint_weight, out_weight, gain_one, shift_one = self_backward(
        hidden_grad, flat, target_ids, True, w_joint, w_out, self_saved
    )
    grads = (
        joint_weight,
        out_weight,
        jnp.concatenate([cross_query_weight, cross_out_weight], axis=1),
        in_weight,
        in_bias,
        back_weight,
        back_bias,
        jnp.stack([gain_one, gain_two, gain_three]),
        jnp.stack([shift_one, shift_two, shift_three]),
    )
    return (
        output.astype(jnp.bfloat16).reshape(rows, length, width),
        token_grad.reshape(rows, length, width),
        keys_grad,
        grads,
    )


def encoder_side(step, micro, inputs, source_ids, params, send_memory, state):
    outputs, token_grads, grads, arrived_keys, arrived_memory, arrived_grads = state
    rows, length, width = inputs.shape[1:]
    out_keys = jnp.zeros((rows, length, 2 * width), jnp.bfloat16)
    out_memory = jnp.zeros((rows, length, width), jnp.bfloat16)
    if step < micro:
        memory_low, unused = encoder_forward(inputs[step], source_ids[step], params)
        outputs = outputs.at[step].set(memory_low.reshape(rows, length, width))
        out_keys = (
            product(memory_low, params[2]).astype(jnp.bfloat16).reshape(rows, length, 2 * width)
        )
    if step >= 2:
        back_step = step - 2
        memory_low, saved = encoder_forward(inputs[back_step], source_ids[back_step], params)
        token_grad, delta = encoder_backward(
            source_ids[back_step], params, memory_low, saved, arrived_keys.reshape(-1, 2 * width)
        )
        token_grads = token_grads.at[back_step].set(token_grad.reshape(rows, length, width))
        grads = tuple((total + extra for total, extra in zip(grads, delta)))
    return (outputs, token_grads, grads, out_keys, out_memory)


def decoder_side(
    step, micro, inputs, source_ids, target_ids, cotangent, params, far_cross, send_memory, state
):
    outputs, token_grads, grads, arrived_keys, arrived_memory, arrived_grads = state
    rows, length, width = inputs.shape[1:]
    out_keys = jnp.zeros((rows, length, 2 * width), jnp.bfloat16)
    out_memory = jnp.zeros((rows, length, width), jnp.bfloat16)
    if 1 <= step <= micro:
        current = step - 1
        output, token_grad, keys_grad, delta = decoder_pass(
            inputs[current],
            target_ids[current],
            source_ids[current],
            arrived_keys,
            cotangent[current],
            params,
        )
        outputs = outputs.at[current].set(output)
        token_grads = token_grads.at[current].set(token_grad)
        grads = tuple((total + extra for total, extra in zip(grads, delta)))
        out_keys = keys_grad
    return (outputs, token_grads, grads, out_keys, out_memory)


def shards(
    layer_input,
    cotangent,
    src_segments,
    tgt_segments,
    attn_qkv,
    attn_out,
    cross_proj,
    ffn_in,
    ffn_in_bias,
    ffn_out,
    ffn_out_bias,
    norm_gain,
    norm_bias,
):
    params = (
        attn_qkv[0],
        attn_out[0],
        cross_proj[0],
        ffn_in[0],
        ffn_in_bias[0],
        ffn_out[0],
        ffn_out_bias[0],
        norm_gain[0],
        norm_bias[0],
    )
    inputs = layer_input[0]
    micro, rows, length, width = inputs.shape
    first_section = lax.axis_index("section") == 0
    far_cross = params[2]
    grads = tuple((jnp.zeros(weight.shape, jnp.float32) for weight in params))
    outputs = jnp.zeros(inputs.shape, jnp.bfloat16)
    token_grads = jnp.zeros(inputs.shape, jnp.float32)
    arrived_keys = jnp.zeros((rows, length, 2 * width), jnp.bfloat16)
    arrived_grads = jnp.zeros((rows, length, 2 * width), jnp.bfloat16)
    arrived_memory = jnp.zeros((rows, length, width), jnp.bfloat16)
    for step in range(micro + 2):
        first_branch = functools.partial(
            encoder_side, step, micro, inputs, src_segments, params, False
        )
        second_branch = functools.partial(
            decoder_side,
            step,
            micro,
            inputs,
            src_segments,
            tgt_segments,
            cotangent,
            params,
            far_cross,
            False,
        )
        state = (outputs, token_grads, grads, arrived_keys, arrived_memory, arrived_grads)
        outputs, token_grads, grads, out_keys, out_memory = lax.cond(
            first_section, first_branch, second_branch, state
        )
        if step <= micro:
            arrived_keys = swapped(out_keys, "section", 0)
    summed = lax.psum(
        (grads[0], grads[1], grads[2], grads[3], grads[4], grads[5], grads[6], grads[7], grads[8]),
        "dp",
    )
    return (outputs[None], token_grads[None]) + tuple((total[None] for total in summed))


def solution(mesh):
    return jax.shard_map(
        shards,
        mesh=mesh,
        in_specs=(
            P("section", None, "dp", None, None),
            P(None, "dp", None, None),
            P(None, "dp", None),
            P(None, "dp", None),
            P("section", None, None),
            P("section", None, None),
            P("section", None, None),
            P("section", None, None),
            P("section", None),
            P("section", None, None),
            P("section", None),
            P("section", None, None),
            P("section", None, None),
        ),
        out_specs=(
            P("section", None, "dp", None, None),
            P("section", None, "dp", None, None),
            P("section", None, None),
            P("section", None, None),
            P("section", None, None),
            P("section", None, None),
            P("section", None),
            P("section", None, None),
            P("section", None),
            P("section", None, None),
            P("section", None, None),
        ),
        check_vma=False,
    )
```

profile of v0, /device:TPU:0, one launch (start us, length us, event | category | flops | bytes accessed | tf_op | source)
XLA Modules:
  0.0 1528.6 jit_solution(12842554586742210800)
XLA Ops:
  8.5 138.2 %conditional.4 = (bf16[2,1,1024,512]{2,3,1,0:T(8,128)(2,1)}, bf16[1,1024,1024]{2,1,0:T(8,128)(2,1)}) conditional(s32[]{:T(128)} %convert_element_type.510, () %tuple.208, (bf16[2,1,1024,512]{3,2,1,0:T(8,128)(2,1)}, bf16[512,1536]{1,0:T(8,128)(2,1)}, s32[2,1,1024]{2,1,0:T(1,128)}, bf16[512,512]{1,0:T(8,128)(2,1)}, f32[3,512]{1,0:T(4,128)}, ...), branch_computations={%region_0.0_spmd, %region_1.12_spmd} | conditional | flops 8783925248 | bytes 154501680 | solution.py:486
  27.1 80.7 %while.267 = (s32[]{:T(128)}, bf16[2,512,512]{2,1,0:T(8,128)(2,1)}, s32[2,512]{1,0:T(2,128)S(1)}, s32[1024]{0:T(1024)S(1)}, bf16[2,512,8,64]{1,3,2,0:T(8,128)(2,...) while((s32[]{:T(128)}, bf16[2,512,512]{2,1,0:T(8,128)(2,1)}, ...), condition=%wide.region_5.5_spmd, body=%wide.region_2.4_spmd.sunk | while | flops 1099957248 | bytes 73443432 | solution.py:105
  37.3 20.6 %fusion.863 = (f32[8,512]{1,0:T(8,128)S(1)}, f32[8,512,1024]{2,1,0:T(8,128)}) fusion(f32[8,512,1024]{2,1,0:T(8,128)} %fusion.862, pred[512,1024]{1,0:T(8,128)(4,1)S(1)} %broadcast_compare_fusion.29), kind=kOutput, calls=%fused_computation.874.clone.1 | output fusion | flops 16778240 | bytes 34095104 | tf_op jit(solution)/shard_map/cond/branch_1_fun/while/body/eval_jaxpr/while/body/eval_jaxpr/sub | solution.py:83
  77.2 20.6 %fusion.863 = (f32[8,512]{1,0:T(8,128)S(1)}, f32[8,512,1024]{2,1,0:T(8,128)}) fusion(f32[8,512,1024]{2,1,0:T(8,128)} %fusion.862, pred[512,1024]{1,0:T(8,128)(4,1)S(1)} %broadcast_compare_fusion.29), kind=kOutput, calls=%fused_computation.874.clone.1 | output fusion | flops 16778240 | bytes 34095104 | tf_op jit(solution)/shard_map/cond/branch_1_fun/while/body/eval_jaxpr/while/body/eval_jaxpr/sub | solution.py:83
  111.5 25.9 %fusion.516 = (f32[1024]{0:T(1024)S(1)}, f32[1024,512]{0,1:T(8,128)S(1)}) fusion(f32[512]{0:T(512)S(1)} %bitcast.1164, bf16[2048,512]{1,0:T(8,128)(2,1)} %get-tuple-element.1243, f32[2048]{0:T(1024)S(1)} %bitcast.1154, bf16[512,2048]{1,0:T(8,128)(2,1)} %get-tuple-element.1241, f32[1024,512]{0,1:T(8,128)} %copy-done.73, f32[512]{0:T(512)S(1)} %bitcast.1112, ...), kind=kOutput, calls=%fused_computation.881 | convolution fusion | flops 4439669760 | bytes 8415232 | tf_op jit(solution)/shard_map/cond/branch_1_fun/dot_general | solution.py:23
  150.9 48.3 %collective-permute-done = bf16[1,1024,1024]{1,2,0:T(8,128)(2,1)} collective-permute-done((bf16[1,1024,1024]{1,2,0:T(8,128)(2,1)}, bf16[1,1024,1024]{1,2,0:T(8,128)(2,1)}, u32[]{:S(2)}, u32[]{:S(2)}) %collective-permute-start) | collective-permute-done | bytes 2097184 | tf_op jit(solution)/shard_map/ppermute | solution.py:19
  199.2 146.0 %conditional.5 = (bf16[2,1,1024,512]{2,3,1,0:T(8,128)(2,1)}, f32[2,1,1024,512]{2,3,1,0:T(8,128)S(1)}, f32[512,1536]{0,1:T(8,128)S(1)}, f32[512,512]{1,0:T(8,128)...) conditional(s32[]{:T(128)} %convert_element_type.510, ...), branch_computations={%region_12.46_spmd, %region_46.57_spmd} | conditional | flops 31637897216 | bytes 1149900544 | solution.py:486
  218.6 80.3 %while.266 = (s32[]{:T(128)}, bf16[2,512,512]{2,1,0:T(8,128)(2,1)}, s32[2,512]{1,0:T(2,128)S(1)}, s32[1024]{0:T(1024)S(1)}, bf16[2,512,8,64]{1,3,2,0:T(8,128)(2,...) while((s32[]{:T(128)}, bf16[2,512,512]{2,1,0:T(8,128)(2,1)}, ...), condition=%wide.region_50.50_spmd, body=%wide.region_47.49_spmd.sunk | while | flops 1099957248 | bytes 73443432 | solution.py:105
  228.3 20.6 %fusion.843 = (f32[8,512]{1,0:T(8,128)S(1)}, f32[8,512,1024]{2,1,0:T(8,128)}) fusion(f32[8,512,1024]{2,1,0:T(8,128)} %fusion.842, pred[512,1024]{1,0:T(8,128)(4,1)S(1)} %broadcast_compare_fusion.26), kind=kOutput, calls=%fused_computation.875.clone.1 | output fusion | flops 16778240 | bytes 34095104 | tf_op jit(solution)/shard_map/cond/branch_1_fun/while/body/eval_jaxpr/while/body/eval_jaxpr/sub | solution.py:83
  302.6 26.1 %fusion.524 = (f32[1024]{0:T(1024)S(1)}, f32[1024,512]{0,1:T(8,128)S(1)}) fusion(f32[512]{0:T(512)S(1)} %bitcast.1166, bf16[2048,512]{1,0:T(8,128)(2,1)} %get-tuple-element.1305, f32[2048]{0:T(1024)S(1)} %bitcast.1157, bf16[512,2048]{1,0:T(8,128)(2,1)} %get-tuple-element.1303, f32[1024,512]{0,1:T(8,128)} %copy-done.74, f32[512]{0:T(512)S(1)} %bitcast.1114, ...), kind=kOutput, calls=%fused_computation.887 | convolution fusion | flops 4439669760 | bytes 8415232 | tf_op jit(solution)/shard_map/cond/branch_1_fun/dot_general | solution.py:23
  345.2 196.0 %collective-permute-start.1 = (bf16[1,1024,1024]{2,1,0:T(8,128)(2,1)}, bf16[1,1024,1024]{2,1,0:T(8,128)(2,1)}, u32[]{:S(2)}, u32[]{:S(2)}) collective-permute-start(bf16[1,1024,1024]{2,1,0:T(8,128)(2,1)} %get-tuple-element.2422), channel_id=1, source_target_pairs={{0,16},{16,0},{1,17},{17,1},{2,18},{18,2},{3,19},{19,3},{4,20},{20... | collective-permute-start | bytes 6291464 | tf_op jit(solution)/shard_map/ppermute | solution.py:19
  541.1 46.0 %collective-permute-done.1 = bf16[1,1024,1024]{2,1,0:T(8,128)(2,1)} collective-permute-done((bf16[1,1024,1024]{2,1,0:T(8,128)(2,1)}, bf16[1,1024,1024]{2,1,0:T(8,128)(2,1)}, u32[]{:S(2)}, u32[]{:S(2)}) %collective-permute-start.1) | collective-permute-done | bytes 2097184 | tf_op jit(solution)/shard_map/ppermute | solution.py:19
  587.1 252.5 %conditional.6 = (f32[2,1,1024,512]{2,3,1,0:T(8,128)}, f32[512,1536]{0,1:T(8,128)}, f32[512,512]{1,0:T(8,128)}, f32[512,1024]{0,1:T(8,128)}, f32[512,2048]{1,0:T...) conditional(s32[]{:T(128)} %convert_element_type.510, ...), branch_computations={%region_57.91_spmd, %region_91.119_spmd} | conditional | flops 31641571328 | bytes 1338777472 | solution.py:486
  615.0 31.6 %while.262 = (s32[]{:T(128)}, bf16[2,512,512]{2,1,0:T(8,128)(2,1)}, f32[2,8,512]{2,1,0:T(8,128)}, s32[2,512]{1,0:T(2,128)S(1)}, s32[1024]{0:T(1024)S(1)}, /*inde...) while((s32[]{:T(128)}, bf16[2,512,512]{2,1,0:T(8,128)(2,1)}, ...), condition=%wide.region_95.95_spmd, body=%wide.region_92.94_spmd.sunk | while | flops 1112535040 | bytes 57813108 | solution.py:105
  649.6 22.6 %multiply_convert_fusion.10 = (bf16[1024,2048]{1,0:T(8,128)(2,1)S(1)}, f32[1024,2048]{1,0:T(8,128)}, f32[1024,2048]{1,0:T(8,128)}) fusion(f32[2048]{0:T(1024)S(1)} %bitcast.1160, bf16[512,2048]{1,0:T(8,128)(2,1)S(1)} %copy-done.257, f32[1024,512]{1,0:T(8,128)S(1)} %get-tuple-element.2844, f32[512]{0:T(512)S(1)} %bitcast.1022, f32[512]{0:T(512)S(1)} %bitcast.1003, ...), kind=kOutput, calls=%fused_computation.693 | convolution fusion | flops 2288517120 | bytes 25186304 | tf_op jit(solution)/shard_map/cond/branch_1_fun/dot_general | solution.py:23
  730.5 88.6 %while.263 = (s32[]{:T(128)}, f32[1024,8,64]{0,2,1:T(8,128)}, f32[1024,8,64]{0,2,1:T(8,128)}, bf16[2,512,512]{2,1,0:T(8,128)(2,1)}, bf16[2,512,8,64]{1,3,2,0:T(8...) while((s32[]{:T(128)}, f32[1024,8,64]{0,2,1:T(8,128)}, ...), condition=%wide.region_110.110_spmd.clone, body=%wide.region_108.109_spmd.clone.sunk | while | flops 2738352128 | bytes 192604496 | solution.py:191
  842.6 110.9 %collective-permute-start.2 = (bf16[1,1024,1024]{2,1,0:T(8,128)(2,1)S(1)}, bf16[1,1024,1024]{2,1,0:T(8,128)(2,1)S(1)}, u32[]{:S(2)}, u32[]{:S(2)}) collective-permute-start(bf16[1,1024,1024]{2,1,0:T(8,128)(2,1)S(1)} %copy.327), channel_id=1, source_target_pairs={{0,16},{16,0},{1,17},{17,1},{2,18},{18,2},{3,19},{19,3},{4,20},{20... | collective-permute-start | bytes 6291464 | tf_op jit(solution)/shard_map/ppermute | solution.py:19
  953.5 44.8 %collective-permute-done.2 = bf16[1,1024,1024]{2,1,0:T(8,128)(2,1)S(1)} collective-permute-done((bf16[1,1024,1024]{2,1,0:T(8,128)(2,1)S(1)}, bf16[1,1024,1024]{2,1,0:T(8,128)(2,1)S(1)}, u32[]{:S(2)}, u32[]{:S(2)}) %collective-permute-start.2) | collective-permute-done | bytes 2097184 | tf_op jit(solution)/shard_map/ppermute | solution.py:19
  999.6 236.8 %conditional.7 = (f32[512,1536]{0,1:T(8,128)}, f32[512,512]{1,0:T(8,128)}, f32[512,1024]{1,0:T(8,128)}, f32[512,2048]{1,0:T(8,128)}, f32[2048]{0:T(1024)}, /*ind...) conditional(s32[]{:T(128)} %convert_element_type.510, ...), branch_computations={%region_119.120_spmd, %region_120.148_spmd} | conditional | flops 25585274880 | bytes 558493184 | solution.py:486
  1020.5 31.6 %while.264 = (s32[]{:T(128)}, bf16[2,512,512]{2,1,0:T(8,128)(2,1)}, f32[2,8,512]{2,1,0:T(8,128)}, s32[2,512]{1,0:T(2,128)S(1)}, s32[1024]{0:T(1024)S(1)}, /*inde...) while((s32[]{:T(128)}, bf16[2,512,512]{2,1,0:T(8,128)(2,1)}, ...), condition=%wide.region_124.124_spmd, body=%wide.region_121.123_spmd.sunk | while | flops 1112535040 | bytes 57813108 | solution.py:105
  1055.1 22.5 %multiply_convert_fusion.11 = (bf16[1024,2048]{1,0:T(8,128)(2,1)S(1)}, f32[1024,2048]{1,0:T(8,128)}, f32[1024,2048]{1,0:T(8,128)}) fusion(f32[2048]{0:T(1024)S(1)} %bitcast.1162, bf16[512,2048]{1,0:T(8,128)(2,1)S(1)} %copy-done.259, f32[1024,512]{1,0:T(8,128)S(1)} %get-tuple-element.2866, f32[512]{0:T(512)S(1)} %bitcast.1019, f32[512]{0:T(512)S(1)} %bitcast.998, ...), kind=kOutput, calls=%fused_computation.780 | convolution fusion | flops 2288517120 | bytes 25186304 | tf_op jit(solution)/shard_map/cond/branch_1_fun/dot_general | solution.py:23
  1130.6 88.5 %while.265 = (s32[]{:T(128)}, f32[1024,8,64]{0,2,1:T(8,128)}, f32[1024,8,64]{0,2,1:T(8,128)}, bf16[2,512,512]{2,1,0:T(8,128)(2,1)}, bf16[2,512,8,64]{1,3,2,0:T(8...) while((s32[]{:T(128)}, f32[1024,8,64]{0,2,1:T(8,128)}, ...), condition=%wide.region_139.139_spmd.clone, body=%wide.region_137.138_spmd.clone.sunk | while | flops 2738352128 | bytes 192604496 | solution.py:191
  1240.7 62.1 %all-reduce.6 = (f32[1,2048]{1,0:T(1,128)}, f32[1,512]{1,0:T(1,128)}, f32[1,3,512]{2,0,1:T(1,128)}, f32[1,3,512]{2,0,1:T(1,128)}) all-reduce(f32[1,2048]{1,0:T(1,128)S(1)} %bitcast.1008, f32[1,512]{1,0:T(1,128)S(1)} %bitcast.1059, f32[1,3,512]{2,0,1:T(1,128)S(1)} %broadcast_in_dim.583, ...), channel_id=1, replica_groups=mesh['section'=2,'dp'=16] {'dp'}, use_global_device_ids=true, to_apply=%region_152.153 | all-reduce | flops 5632 | bytes 45056 | tf_op jit(solution)/shard_map/psum | solution.py:491
  1302.9 205.7 %all-reduce.10.cloned.1.call-done = (f32[1,512,1536]{2,1,0:T(8,128)}, f32[1,512,512]{2,1,0:T(8,128)}, f32[1,512,1024]{2,1,0:T(8,128)}, f32[1,512,2048]{2,1,0:T(8,128)}, f32[1,2048,512]{2,1,0:T(8,128)}) async-done(((f32[1,512,1536]{2,1,0:T(8,128)}, f32[1,512,512]{2,1,0:T(8,128)}, f32[1,512,1024]{2,1,0:T(8,128)}, f32[1,512,2048]{2,1,0:T(8,128)}, f32[1,2048,512]{2,1,0:T(8,128)}), (f32[1,512,1536]{2,1,0:T(8,128)}, ...) | async-done | bytes 14680080 | tf_op jit(solution)/shard_map/psum | solution.py:491
  (556 shorter events, 622.6 us)
Async XLA Ops:
  7.2 1501.4 %all-reduce.10.cloned.1.call-start = ((), (), s32[]{:S(2)}) async-start(), calls=%async_computation | async-start | bytes 29360128 | tf_op jit(solution)/shard_map/psum | solution.py:491
  27.1 80.7 %copy-start.45 = (bf16[512,512]{1,0:T(8,128)(2,1)S(1)}, bf16[512,512]{1,0:T(8,128)(2,1)}, u32[]{:S(2)}) copy-start(bf16[512,512]{1,0:T(8,128)(2,1)} %get-tuple-element.1238) | copy-start | bytes 1572868 | tf_op jit(solution)/shard_map/cond
  111.5 26.7 %copy-start.203 = (f32[1,512]{1,0:T(1,128)S(1)}, f32[1,512]{1,0:T(1,128)}, u32[]{:S(2)}) copy-start(f32[1,512]{1,0:T(1,128)} %get-tuple-element.2712) | copy-start | bytes 6148 | tf_op jit(solution)/shard_map/cond
  111.5 26.7 %copy-start.204 = (f32[1,512]{1,0:T(1,128)S(1)}, f32[1,512]{1,0:T(1,128)}, u32[]{:S(2)}) copy-start(f32[1,512]{1,0:T(1,128)} %get-tuple-element.2726) | copy-start | bytes 6148 | tf_op jit(solution)/shard_map/cond
  146.7 52.4 %copy-start.24 = (bf16[1,2,1,1024,512]{4,3,2,1,0:T(8,128)(2,1)S(1)}, bf16[1,2,1,1024,512]{4,3,2,1,0:T(8,128)(2,1)}, u32[]{:S(2)}) copy-start(bf16[1,2,1,1024,512]{4,3,2,1,0:T(8,128)(2,1)} %param.81) | copy-start | bytes 6291460
  146.7 52.4 %copy-start.165 = (s32[2,1,1024]{2,1,0:T(1,128)S(1)}, s32[2,1,1024]{2,1,0:T(1,128)}, u32[]{:S(2)}) copy-start(s32[2,1,1024]{2,1,0:T(1,128)} %param.83) | copy-start | bytes 24580
  146.8 52.4 %copy-start.200 = (s32[2,1,1024]{2,1,0:T(1,128)S(1)}, s32[2,1,1024]{2,1,0:T(1,128)}, u32[]{:S(2)}) copy-start(s32[2,1,1024]{2,1,0:T(1,128)} %param.84) | copy-start | bytes 24580
  150.9 48.3 %collective-permute-start = (bf16[1,1024,1024]{1,2,0:T(8,128)(2,1)}, bf16[1,1024,1024]{1,2,0:T(8,128)(2,1)}, u32[]{:S(2)}, u32[]{:S(2)}) collective-permute-start(bf16[1,1024,1024]{1,2,0:T(8,128)(2,1)} %copy.316), channel_id=1, source_target_pairs={{0,16},{16,0},{1,17},{17,1},{2,18},{18,2},{3,19},{19,3},{4,20},{20... | collective-permute-start | bytes 6291464 | tf_op jit(solution)/shard_map/ppermute | solution.py:19
  218.6 80.3 %copy-start.48 = (bf16[512,512]{1,0:T(8,128)(2,1)S(1)}, bf16[512,512]{1,0:T(8,128)(2,1)}, u32[]{:S(2)}) copy-start(bf16[512,512]{1,0:T(8,128)(2,1)} %get-tuple-element.1300) | copy-start | bytes 1572868 | tf_op jit(solution)/shard_map/cond
  302.6 26.6 %copy-start.201 = (f32[1,512]{1,0:T(1,128)S(1)}, f32[1,512]{1,0:T(1,128)}, u32[]{:S(2)}) copy-start(f32[1,512]{1,0:T(1,128)} %get-tuple-element.2730) | copy-start | bytes 6148 | tf_op jit(solution)/shard_map/cond
  302.6 26.6 %copy-start.202 = (f32[1,512]{1,0:T(1,128)S(1)}, f32[1,512]{1,0:T(1,128)}, u32[]{:S(2)}) copy-start(f32[1,512]{1,0:T(1,128)} %get-tuple-element.2744) | copy-start | bytes 6148 | tf_op jit(solution)/shard_map/cond
  345.1 242.0 %copy-start.37 = (f32[2,1,1024,512]{2,3,1,0:T(8,128)}, f32[2,1,1024,512]{2,3,1,0:T(8,128)S(1)}, u32[]{:S(2)}) copy-start(f32[2,1,1024,512]{2,3,1,0:T(8,128)S(1)} %get-tuple-element.1516) | copy-start | bytes 12582916
  345.1 242.0 %copy-start.177 = (f32[3,512]{1,0:T(4,128)}, f32[3,512]{1,0:T(4,128)S(1)}, u32[]{:S(2)}) copy-start(f32[3,512]{1,0:T(4,128)S(1)} %get-tuple-element.1524) | copy-start | bytes 18436
  345.2 242.0 %copy-start.288 = (f32[512,1536]{0,1:T(8,128)}, f32[512,1536]{0,1:T(8,128)S(1)}, u32[]{:S(2)}) copy-start(f32[512,1536]{0,1:T(8,128)S(1)} %get-tuple-element.1517) | copy-start | bytes 9437188
  345.2 241.9 %collective-permute-start.1 = (bf16[1,1024,1024]{2,1,0:T(8,128)(2,1)}, bf16[1,1024,1024]{2,1,0:T(8,128)(2,1)}, u32[]{:S(2)}, u32[]{:S(2)}) collective-permute-start(bf16[1,1024,1024]{2,1,0:T(8,128)(2,1)} %get-tuple-element.2422), channel_id=1, source_target_pairs={{0,16},{16,0},{1,17},{17,1},{2,18},{18,2},{3,19},{19,3},{4,20},{20... | collective-permute-start | bytes 6291464 | tf_op jit(solution)/shard_map/ppermute | solution.py:19
  615.0 31.6 %copy-start.51 = (bf16[512,512]{1,0:T(8,128)(2,1)S(1)}, bf16[512,512]{1,0:T(8,128)(2,1)}, u32[]{:S(2)}) copy-start(bf16[512,512]{1,0:T(8,128)(2,1)} %get-tuple-element.1388) | copy-start | bytes 1572868 | tf_op jit(solution)/shard_map/cond
  649.1 23.1 %copy-start.40 = (f32[1024,512]{1,0:T(8,128)}, f32[1024,512]{1,0:T(8,128)S(1)}, u32[]{:S(2)}) copy-start(f32[1024,512]{1,0:T(8,128)S(1)} %get-tuple-element.2844) | copy-start | bytes 6291460 | tf_op jit(solution)/shard_map/cond
  649.6 22.6 %copy-start.263 = (bf16[2048,512]{1,0:T(8,128)(2,1)S(1)}, bf16[2048,512]{1,0:T(8,128)(2,1)}, u32[]{:S(2)}) copy-start(bf16[2048,512]{1,0:T(8,128)(2,1)} %get-tuple-element.1392) | copy-start | bytes 6291460 | tf_op jit(solution)/shard_map/cond
  649.6 22.6 %copy-start.284 = (f32[1,512]{1,0:T(1,128)S(1)}, f32[1,512]{1,0:T(1,128)}, u32[]{:S(2)}) copy-start(f32[1,512]{1,0:T(1,128)} %get-tuple-element.1393) | copy-start | bytes 6148 | tf_op jit(solution)/shard_map/cond
  839.7 159.9 %copy-start.166 = (s32[2,1,1024]{2,1,0:T(1,128)S(1)}, s32[2,1,1024]{2,1,0:T(1,128)}, u32[]{:S(2)}) copy-start(s32[2,1,1024]{2,1,0:T(1,128)} %param.83) | copy-start | bytes 24580
  842.6 155.7 %collective-permute-start.2 = (bf16[1,1024,1024]{2,1,0:T(8,128)(2,1)S(1)}, bf16[1,1024,1024]{2,1,0:T(8,128)(2,1)S(1)}, u32[]{:S(2)}, u32[]{:S(2)}) collective-permute-start(bf16[1,1024,1024]{2,1,0:T(8,128)(2,1)S(1)} %copy.327), channel_id=1, source_target_pairs={{0,16},{16,0},{1,17},{17,1},{2,18},{18,2},{3,19},{19,3},{4,20},{20... | collective-permute-start | bytes 6291464 | tf_op jit(solution)/shard_map/ppermute | solution.py:19
  1020.5 31.6 %copy-start.52 = (bf16[512,512]{1,0:T(8,128)(2,1)S(1)}, bf16[512,512]{1,0:T(8,128)(2,1)}, u32[]{:S(2)}) copy-start(bf16[512,512]{1,0:T(8,128)(2,1)} %get-tuple-element.1448) | copy-start | bytes 1572868 | tf_op jit(solution)/shard_map/cond
  1055.1 22.5 %copy-start.265 = (bf16[2048,512]{1,0:T(8,128)(2,1)S(1)}, bf16[2048,512]{1,0:T(8,128)(2,1)}, u32[]{:S(2)}) copy-start(bf16[2048,512]{1,0:T(8,128)(2,1)} %get-tuple-element.1452) | copy-start | bytes 6291460 | tf_op jit(solution)/shard_map/cond
  1055.1 22.5 %copy-start.285 = (f32[1,512]{1,0:T(1,128)S(1)}, f32[1,512]{1,0:T(1,128)}, u32[]{:S(2)}) copy-start(f32[1,512]{1,0:T(1,128)} %get-tuple-element.1453) | copy-start | bytes 6148 | tf_op jit(solution)/shard_map/cond
  (110 other events, 399.6 us)
Sparse Core Ops, SparseCore 0:
  1240.1 268.4 all-reduce.9
where the time goes:
time: 1540 us; the launch traced here: 1530 us
  matrix products  454 us (29%)
  waiting for transfers between devices  345 us (22%)
  starting transfers between devices  307 us (20%)
  other arithmetic  175 us (11%)
  local copies, waits for them, and re-layouts  152 us (10%)
  blocking collectives  62.1 us (4%)
  loops' own time  18.8 us (1%)
    ppermute x3, starting transfers between devices, swapped(): return lax.ppermute(value, axis, pairs)  307 us
    psum x1, waiting for transfers between devices, shards(): lax.psum((grads[0], grads[1], grads[2], grads[3], grads[4], grads[5], gra...  206 us
    ppermute x3, waiting for transfers between devices, swapped(): return lax.ppermute(value, axis, pairs)  139 us
    dot_general x16, matrix products, product(): return jnp.dot(left, right, preferred_element_type=jnp.float32)  131 us
    sub x4, other arithmetic, one_block(): raised = jnp.exp(scores - highest)  82.4 us
    dot_general x12, matrix products, block_scores(): jnp.einsum('qhd,khd->hqk', scaled_query, key_heads, preferred_element_typ...  62.2 us
    psum x1, blocking collectives, shards(): lax.psum((grads[0], grads[1], grads[2], grads[3], grads[4], grads[5], gra...  62.1 us
    dot_general x8, matrix products, one_block(): jnp.einsum('hqk,khd->qhd', weights, value_heads[:limit], preferred_elemen...  59.5 us
  transfers between devices with their start and end apart: 4, of which 4 were waited for; matrix products, arithmetic and copies ran while one was open for 0% of the time, Pallas kernels for 0%

commit v1 on v0

v1 whole, which is shorter than its diff:
```python
import functools
import math

import jax
import jax.numpy as jnp
from jax import lax
from jax.experimental import pallas as pl
from jax.experimental.pallas import tpu as pltpu
from jax.sharding import PartitionSpec as P

HEADS = 8
EPSILON = 1e-05
NEGATIVE = -1000000000.0
BF = jnp.bfloat16
F32 = jnp.float32
LOG2E = 1.4426950408889634
QB = 256
CK = 128
TB = 256
VMEM_LIMIT = 60 * 1024 * 1024


def dot(left, right, lc=1, rc=0):
    return lax.dot_general(
        left, right, (((lc,), (rc,)), ((), ())), preferred_element_type=F32
    )


def norm_stats(value):
    centered = value - jnp.mean(value, axis=-1, keepdims=True)
    spread = jnp.mean(centered * centered, axis=-1, keepdims=True)
    scale = lax.rsqrt(spread + EPSILON)
    return centered * scale, scale


def norm_back(out_grad, unit, scale, gain):
    gain_grad = jnp.sum(out_grad * unit, axis=0, keepdims=True)
    shift_grad = jnp.sum(out_grad, axis=0, keepdims=True)
    inner = out_grad * gain
    mean_one = jnp.mean(inner, axis=-1, keepdims=True)
    mean_two = jnp.mean(inner * unit, axis=-1, keepdims=True)
    return scale * (inner - mean_one - unit * mean_two), gain_grad, shift_grad


def gelu_pair(u):
    phi = 0.5 + 0.5 * lax.erf(u * (1.0 / math.sqrt(2.0)))
    bell = jnp.exp(-0.5 * u * u) * (1.0 / math.sqrt(2.0 * math.pi))
    return u * phi, phi + u * bell


def key_codes(ids_row, length):
    column = jnp.broadcast_to(ids_row.astype(F32), (128, length)).T
    lane = lax.broadcasted_iota(jnp.int32, (length, 128), 1)
    spot = jnp.where(lane < 64, lane, lane - 64)
    codes = jnp.where(
        spot < 4,
        jnp.where(column == spot.astype(F32), 0.0, NEGATIVE),
        jnp.where(spot < 7, -1.0, 0.0),
    )
    return codes, lane < 64


def fill_keys(dst, keys_ref, codes, low_half):
    for pair in range(HEADS // 2):
        slab = keys_ref[:, pair * 128 : pair * 128 + 128].astype(F32)
        dst[2 * pair] = jnp.where(low_half, slab, codes).astype(BF)
        dst[2 * pair + 1] = jnp.where(low_half, codes, slab).astype(BF)


def query_rows(head):
    return (0, 64) if head % 2 == 0 else (64, 0)


def attend_loop(tab_ref, qaug, kaug, vt, attT_ref, lse_ref, oacc, mrow, lrow, length):
    for qb in range(length // QB):
        q = slice(qb * QB, qb * QB + QB)
        oacc[...] = jnp.zeros_like(oacc)
        mrow[...] = jnp.full_like(mrow, -3e38)
        lrow[...] = jnp.zeros_like(lrow)

        def step(kc, masked):
            k0 = pl.multiple_of(kc * CK, CK)
            ks = pl.ds(k0, CK)
            if masked:
                key_pos = k0 + lax.broadcasted_iota(jnp.int32, (CK, QB), 0)
                query_pos = qb * QB + lax.broadcasted_iota(jnp.int32, (CK, QB), 1)
                allowed = key_pos <= query_pos
            for h in range(HEADS):
                s = dot(kaug[h, ks, :], qaug[h, :, q])
                if masked:
                    s = jnp.where(allowed, s, NEGATIVE)
                m_old = mrow[h : h + 1, :]
                m_new = jnp.maximum(m_old, jnp.max(s, axis=0, keepdims=True))
                alpha = jnp.exp2(m_old - m_new)
                p = jnp.exp2(s - m_new)
                lrow[h : h + 1, :] = lrow[h : h + 1, :] * alpha + jnp.sum(
                    p, axis=0, keepdims=True
                )
                mrow[h : h + 1, :] = m_new
                hs = slice(h * 64, h * 64 + 64)
                oacc[hs, :] = oacc[hs, :] * alpha + dot(vt[hs, ks], p.astype(BF))

        @pl.loop(tab_ref[qb, 0], tab_ref[qb, 1])
        def _(kc):
            step(kc, False)

        @pl.loop(tab_ref[qb, 1], tab_ref[qb, 2])
        def _(kc):
            step(kc, True)

        for h in range(HEADS):
            hs = slice(h * 64, h * 64 + 64)
            attT_ref[hs, q] = (oacc[hs, :] * (1.0 / lrow[h : h + 1, :])).astype(BF)
        lse_ref[:, q] = mrow[...] + jnp.log2(lrow[...])


def query_codes(ids_row, length):
    row = lax.broadcasted_iota(jnp.int32, (16, length), 0)
    return jnp.where(row == jnp.broadcast_to(ids_row, (16, length)), 1.0, 0.0), row


def fill_queries(qaug, qT_ref, codes, row, lse_ref, length):
    for h in range(HEADS):
        a, b = query_rows(h)
        qaug[h, a : a + 64, :] = qT_ref[h * 64 : h * 64 + 64, :]
        extra = codes
        if lse_ref is not None:
            lse = lse_ref[h : h + 1, :]
            hi = lse.astype(BF).astype(F32)
            mid = (lse - hi).astype(BF).astype(F32)
            low = lse - hi - mid
            extra = jnp.where(row == 4, hi, jnp.where(row == 5, mid, jnp.where(row == 6, low, codes)))
        qaug[h, b : b + 16, :] = extra.astype(BF)
        qaug[h, b + 16 : b + 64, :] = jnp.zeros((48, length), BF)


def project_queries(src_ref, w_ref, qT_ref, length, width):
    @pl.loop(0, length // TB)
    def _(t):
        rows = pl.ds(pl.multiple_of(t * TB, TB), TB)
        q = dot(src_ref[rows, :], w_ref[:, :width]) * (0.125 * LOG2E)
        qT_ref[:, rows] = q.T.astype(BF)


def out_and_norm(attT_ref, w_ref, resid_ref, ln_ref, res_ref, hid_ref, length):
    @pl.loop(0, length // TB)
    def _(t):
        rows = pl.ds(pl.multiple_of(t * TB, TB), TB)
        a = dot(attT_ref[:, rows], w_ref[...], 0, 0)
        r = resid_ref[rows, :].astype(F32) + a
        res_ref[rows, :] = r.astype(BF)
        unit, _ = norm_stats(r)
        hid_ref[rows, :] = (unit * ln_ref[0:1, :] + ln_ref[1:2, :]).astype(BF)


def self_fwd_kernel(tab_ref, x_ref, ids_ref, w_ref, wout_ref, ln_ref,
                    qT_ref, k_ref, v_ref, attT_ref, lse_ref, res_ref, hid_ref,
                    kaug, qaug, vt, oacc, mrow, lrow):
    length, width = x_ref.shape
    project_queries(x_ref, w_ref, qT_ref, length, width)

    @pl.loop(0, length // TB)
    def _(t):
        rows = pl.ds(pl.multiple_of(t * TB, TB), TB)
        k_ref[rows, :] = dot(x_ref[rows, :], w_ref[:, width : 2 * width]).astype(BF)
        v = dot(x_ref[rows, :], w_ref[:, 2 * width :])
        v_ref[rows, :] = v.astype(BF)
        vt[:, rows] = v.T.astype(BF)

    codes, low_half = key_codes(ids_ref[...], length)
    fill_keys(kaug, k_ref, codes, low_half)
    qcodes, row = query_codes(ids_ref[...], length)
    fill_queries(qaug, qT_ref, qcodes, row, None, length)
    attend_loop(tab_ref, qaug, kaug, vt, attT_ref, lse_ref, oacc, mrow, lrow, length)
    out_and_norm(attT_ref, wout_ref, x_ref, ln_ref, res_ref, hid_ref, length)


def cross_fwd_kernel(tab_ref, h_ref, kv_ref, qids_ref, kids_ref, w_ref, ln_ref,
                     qT_ref, attT_ref, lse_ref, res_ref, hid_ref,
                     kaug, qaug, vt, oacc, mrow, lrow):
    length, width = h_ref.shape
    project_queries(h_ref, w_ref, qT_ref, length, width)

    @pl.loop(0, length // TB)
    def _(t):
        rows = pl.ds(pl.multiple_of(t * TB, TB), TB)
        vt[:, rows] = kv_ref[rows, width:].astype(F32).T.astype(BF)

    codes, low_half = key_codes(kids_ref[...], length)
    fill_keys(kaug, kv_ref, codes, low_half)
    qcodes, row = query_codes(qids_ref[...], length)
    fill_queries(qaug, qT_ref, qcodes, row, None, length)
    attend_loop(tab_ref, qaug, kaug, vt, attT_ref, lse_ref, oacc, mrow, lrow, length)
    out_and_norm(attT_ref, w_ref.at[:, width:], h_ref, ln_ref, res_ref, hid_ref, length)


def attend_back_loop(tab_ref, qaug, kaug, kt, vaug, doaug, jgT, qoff, koff, voff, dqacc, length):
    for qb in range(length // QB):
        q = slice(qb * QB, qb * QB + QB)
        dqacc[...] = jnp.zeros_like(dqacc)

        def step(kc, masked):
            k0 = pl.multiple_of(kc * CK, CK)
            ks = pl.ds(k0, CK)
            if masked:
                key_pos = k0 + lax.broadcasted_iota(jnp.int32, (CK, QB), 0)
                query_pos = qb * QB + lax.broadcasted_iota(jnp.int32, (CK, QB), 1)
                allowed = key_pos <= query_pos
            for h in range(HEADS):
                a, _ = query_rows(h)
                hs = slice(h * 64, h * 64 + 64)
                s = dot(kaug[h, ks, :], qaug[h, :, q])
                if masked:
                    s = jnp.where(allowed, s, NEGATIVE)
                p = jnp.exp2(s)
                dp = dot(vaug[h, ks, :], doaug[h, :, q])
                ds = (p * dp).astype(BF)
                pb = p.astype(BF)
                dqacc[hs, :] += dot(kt[hs, ks], ds)
                jgT[voff + h * 64 : voff + h * 64 + 64, ks] += dot(doaug[h, a : a + 64, q], pb, 1, 1)
                jgT[koff + h * 64 : koff + h * 64 + 64, ks] += dot(qaug[h, a : a + 64, q], ds, 1, 1)

        @pl.loop(tab_ref[qb, 0], tab_ref[qb, 1])
        def _(kc):
            step(kc, False)

        @pl.loop(tab_ref[qb, 1], tab_ref[qb, 2])
        def _(kc):
            step(kc, True)

        jgT[qoff : qoff + 512, q] = dqacc[...] * 0.125


def prepare_back(dr_ref, w_out, attT_ref, doT, doaug, length):
    @pl.loop(0, length // TB)
    def _(t):
        rows = pl.ds(pl.multiple_of(t * TB, TB), TB)
        doT[:, rows] = dot(w_out, dr_ref[rows, :], 1, 1).astype(BF)

    row = lax.broadcasted_iota(jnp.int32, (16, length), 0)
    for h in range(HEADS):
        a, b = query_rows(h)
        hs = slice(h * 64, h * 64 + 64)
        doh = doT[hs, :]
        doaug[h, a : a + 64, :] = doh
        delta = jnp.sum(doh.astype(F32) * attT_ref[hs, :].astype(F32), axis=0, keepdims=True)
        hi = delta.astype(BF).astype(F32)
        mid = (delta - hi).astype(BF).astype(F32)
        low = delta - hi - mid
        extra = jnp.where(row == 4, hi, jnp.where(row == 5, mid, jnp.where(row == 6, low, 0.0)))
        doaug[h, b : b + 16, :] = extra.astype(BF)
        doaug[h, b + 16 : b + 64, :] = jnp.zeros((48, length), BF)


def prepare_keys(keys_ref, values_ref, codes, low_half, kaug, kt, vaug, length):
    fill_keys(kaug, keys_ref, codes, low_half)
    fill_keys(vaug, values_ref, jnp.where(codes == NEGATIVE, 0.0, codes), low_half)

    @pl.loop(0, length // TB)
    def _(t):
        rows = pl.ds(pl.multiple_of(t * TB, TB), TB)
        kt[:, rows] = keys_ref[rows, :].astype(F32).T.astype(BF)


def finish_grads(jgT, jg, koff, length):
    rows_total = jgT.shape[0]
    for r in range(0, rows_total, 512):
        f = math.log(2.0) if r == koff else 1.0
        jg[r : r + 512, :] = (jgT[r : r + 512, :] * f).astype(BF)


def self_bwd_kernel(tab_ref, dh_ref, res_ref, x_ref, ids_ref, qT_ref, k_ref, v_ref, attT_ref,
                    lse_ref, w_ref, wout_ref, ln_ref,
                    dx_ref, dwT_ref, dwout_ref, dln_ref,
                    kaug, kt, vaug, qaug, doaug, doT, dqacc, jgT, jg, dr):
    length, width = x_ref.shape
    dln_ref[...] = jnp.zeros_like(dln_ref)

    @pl.loop(0, length // TB)
    def _(t):
        rows = pl.ds(pl.multiple_of(t * TB, TB), TB)
        unit, scale = norm_stats(res_ref[rows, :].astype(F32))
        d, gg, sg = norm_back(dh_ref[rows, :].astype(F32), unit, scale, ln_ref[0:1, :])
        dln_ref[0:1, :] += gg
        dln_ref[1:2, :] += sg
        dr[rows, :] = d.astype(BF)

    dwout_ref[...] = dot(attT_ref[...], dr[...]).astype(BF)
    prepare_back(dr, wout_ref[...], attT_ref, doT, doaug, length)
    codes, low_half = key_codes(ids_ref[...], length)
    prepare_keys(k_ref, v_ref, codes, low_half, kaug, kt, vaug, length)
    qcodes, row = query_codes(ids_ref[...], length)
    fill_queries(qaug, qT_ref, qcodes, row, lse_ref, length)
    jgT[width:, :] = jnp.zeros((2 * width, length), F32)
    attend_back_loop(tab_ref, qaug, kaug, kt, vaug, doaug, jgT, 0, width, 2 * width, dqacc, length)
    finish_grads(jgT, jg, width, length)
    @pl.loop(0, 3 * width // TB)
    def _(t):
        rows = pl.ds(pl.multiple_of(t * TB, TB), TB)
        dwT_ref[rows, :] = dot(jg[rows, :], x_ref[...]).astype(BF)

    @pl.loop(0, length // TB)
    def _(t):
        rows = pl.ds(pl.multiple_of(t * TB, TB), TB)
        d = dot(jg[:, rows], w_ref[...], 0, 1)
        dx_ref[rows, :] = (dr[rows, :].astype(F32) + d).astype(dx_ref.dtype)


def cross_bwd_kernel(tab_ref, dr_ref, h_ref, mem_ref, qids_ref, kids_ref, qT_ref, kv_ref, attT_ref,
                     lse_ref, w_ref, wkv_ref,
                     dh_ref, dmem_ref, dwqT_ref, dwo_ref, dwkvT_ref,
                     kaug, kt, vaug, qaug, doaug, doT, dqacc, jgT, jg):
    length, width = h_ref.shape
    dwo_ref[...] = dot(attT_ref[...], dr_ref[...]).astype(BF)
    prepare_back(dr_ref, w_ref[:, width:], attT_ref, doT, doaug, length)
    codes, low_half = key_codes(kids_ref[...], length)
    prepare_keys(kv_ref.at[:, :width], kv_ref.at[:, width:], codes, low_half, kaug, kt, vaug, length)
    qcodes, row = query_codes(qids_ref[...], length)
    fill_queries(qaug, qT_ref, qcodes, row, lse_ref, length)
    jgT[width:, :] = jnp.zeros((2 * width, length), F32)
    attend_back_loop(tab_ref, qaug, kaug, kt, vaug, doaug, jgT, 0, width, 2 * width, dqacc, length)
    finish_grads(jgT, jg, width, length)
    dwqT_ref[...] = dot(jg[:width, :], h_ref[...]).astype(BF)
    @pl.loop(0, 2 * width // TB)
    def _(t):
        at = pl.multiple_of(t * TB, TB)
        dwkvT_ref[pl.ds(at, TB), :] = dot(jg[pl.ds(at + width, TB), :], mem_ref[...]).astype(BF)

    @pl.loop(0, length // TB)
    def _(t):
        rows = pl.ds(pl.multiple_of(t * TB, TB), TB)
        d = dot(jg[:width, rows], w_ref[:, :width], 0, 1)
        dh_ref[rows, :] = (dr_ref[rows, :].astype(F32) + d).astype(BF)
        dmem_ref[rows, :] = dot(jg[width:, rows], wkv_ref[...], 0, 1).astype(BF)


def enc_ffn_fwd_kernel(e1_ref, win_ref, bin_ref, wout_ref, bout_ref, ln_ref, wkv_ref,
                       g_ref, gp_ref, r_ref, mem_ref, kv_ref):
    length, width = e1_ref.shape
    ff = win_ref.shape[1]

    @pl.loop(0, length // TB)
    def _(t):
        rows = pl.ds(pl.multiple_of(t * TB, TB), TB)
        e1 = e1_ref[rows, :]
        total = e1.astype(F32) + bout_ref[...]
        for j in range(0, ff, 512):
            u = dot(e1, win_ref[:, j : j + 512]) + bin_ref[:, j : j + 512]
            g, gp = gelu_pair(u)
            gb = g.astype(BF)
            g_ref[rows, j : j + 512] = gb
            gp_ref[rows, j : j + 512] = gp.astype(BF)
            total += dot(gb, wout_ref[j : j + 512, :])
        r_ref[rows, :] = total.astype(BF)
        unit, _ = norm_stats(total)
        e2 = unit * ln_ref[0:1, :] + ln_ref[1:2, :]
        unit, _ = norm_stats(e2)
        mem = (unit * ln_ref[2:3, :] + ln_ref[3:4, :]).astype(BF)
        mem_ref[rows, :] = mem
        kv_ref[rows, :] = dot(mem, wkv_ref[...]).astype(BF)


def weight_grads(act_ref, du_ref, df_ref, g_ref, dwin_ref, dwoutT_ref):
    ff = du_ref.shape[1]

    @pl.loop(0, ff // TB)
    def _(t):
        cols = pl.ds(pl.multiple_of(t * TB, TB), TB)
        dwin_ref[:, cols] = dot(act_ref[...], du_ref[:, cols], 0, 0).astype(BF)
        dwoutT_ref[:, cols] = dot(df_ref[...], g_ref[:, cols], 0, 0).astype(BF)


def enc_ffn_bwd_kernel(dmem_ref, r_ref, g_ref, gp_ref, e1_ref, win_ref, wout_ref, ln_ref,
                       de1_ref, dwin_ref, dwoutT_ref, dln_ref, dbin_ref, dbout_ref,
                       du_ref, df_ref):
    length, width = e1_ref.shape
    ff = win_ref.shape[1]
    dln_ref[...] = jnp.zeros_like(dln_ref)
    dbin_ref[...] = jnp.zeros_like(dbin_ref)
    dbout_ref[...] = jnp.zeros_like(dbout_ref)

    @pl.loop(0, length // TB)
    def _(t):
        rows = pl.ds(pl.multiple_of(t * TB, TB), TB)
        unit2, scale2 = norm_stats(r_ref[rows, :].astype(F32))
        e2 = unit2 * ln_ref[0:1, :] + ln_ref[1:2, :]
        unit3, scale3 = norm_stats(e2)
        de2, gg, sg = norm_back(dmem_ref[rows, :].astype(F32), unit3, scale3, ln_ref[2:3, :])
        dln_ref[2:3, :] += gg
        dln_ref[3:4, :] += sg
        dr, gg, sg = norm_back(de2, unit2, scale2, ln_ref[0:1, :])
        dln_ref[0:1, :] += gg
        dln_ref[1:2, :] += sg
        df = dr.astype(BF)
        df_ref[rows, :] = df
        dbout_ref[...] += jnp.sum(df.astype(F32), axis=0, keepdims=True)
        total = dr
        for j in range(0, ff, 512):
            dg = dot(df, wout_ref[j : j + 512, :], 1, 1)
            du = dg * gp_ref[rows, j : j + 512].astype(F32)
            dub = du.astype(BF)
            du_ref[rows, j : j + 512] = dub
            dbin_ref[:, j : j + 512] += jnp.sum(du, axis=0, keepdims=True)
            total += dot(dub, win_ref[:, j : j + 512], 1, 1)
        de1_ref[rows, :] = total.astype(BF)

    weight_grads(e1_ref, du_ref, df_ref, g_ref, dwin_ref, dwoutT_ref)


def dec_ffn_kernel(h_ref, res_ref, cot_ref, win_ref, bin_ref, wout_ref, bout_ref, ln_ref,
                   out_ref, dres_ref, dwin_ref, dwoutT_ref, dln_ref, dbin_ref, dbout_ref,
                   g_ref, gp_ref, du_ref, df_ref):
    length, width = h_ref.shape
    ff = win_ref.shape[1]
    dln_ref[...] = jnp.zeros_like(dln_ref)
    dbin_ref[...] = jnp.zeros_like(dbin_ref)
    dbout_ref[...] = jnp.zeros_like(dbout_ref)

    @pl.loop(0, length // TB)
    def _(t):
        rows = pl.ds(pl.multiple_of(t * TB, TB), TB)
        h = h_ref[rows, :]
        total = h.astype(F32) + bout_ref[...]
        for j in range(0, ff, 512):
            u = dot(h, win_ref[:, j : j + 512]) + bin_ref[:, j : j + 512]
            g, gp = gelu_pair(u)
            gb = g.astype(BF)
            g_ref[rows, j : j + 512] = gb
            gp_ref[:, j : j + 512] = gp.astype(BF)
            total += dot(gb, wout_ref[j : j + 512, :])
        unit3, scale3 = norm_stats(total)
        out_ref[rows, :] = (unit3 * ln_ref[2:3, :] + ln_ref[3:4, :]).astype(BF)
        dr, gg, sg = norm_back(cot_ref[rows, :].astype(F32), unit3, scale3, ln_ref[2:3, :])
        dln_ref[2:3, :] += gg
        dln_ref[3:4, :] += sg
        df = dr.astype(BF)
        df_ref[rows, :] = df
        dbout_ref[...] += jnp.sum(df.astype(F32), axis=0, keepdims=True)
        total = dr
        for j in range(0, ff, 512):
            dg = dot(df, wout_ref[j : j + 512, :], 1, 1)
            du = dg * gp_ref[:, j : j + 512].astype(F32)
            dub = du.astype(BF)
            du_ref[rows, j : j + 512] = dub
            dbin_ref[:, j : j + 512] += jnp.sum(du, axis=0, keepdims=True)
            total += dot(dub, win_ref[:, j : j + 512], 1, 1)
        unit2, scale2 = norm_stats(res_ref[rows, :].astype(F32))
        d, gg, sg = norm_back(total, unit2, scale2, ln_ref[0:1, :])
        dln_ref[0:1, :] += gg
        dln_ref[1:2, :] += sg
        dres_ref[rows, :] = d.astype(BF)

    weight_grads(h_ref, du_ref, df_ref, g_ref, dwin_ref, dwoutT_ref)


def call(kernel, outs, scratch, flops, n_smem, *args):
    vm = pl.BlockSpec(memory_space=pltpu.VMEM)
    return pl.pallas_call(
        kernel,
        out_shape=[jax.ShapeDtypeStruct(s, d) for s, d in outs],
        in_specs=[pl.BlockSpec(memory_space=pltpu.SMEM)] * n_smem + [vm] * (len(args) - n_smem),
        out_specs=[vm] * len(outs),
        scratch_shapes=scratch,
        compiler_params=pltpu.CompilerParams(vmem_limit_bytes=VMEM_LIMIT),
        cost_estimate=pl.CostEstimate(flops=flops, bytes_accessed=8 << 20, transcendentals=0),
        name=kernel.__name__,
    )(*args)


def fwd_scratch(n, w):
    return [
        pltpu.VMEM((HEADS, n, 128), BF),
        pltpu.VMEM((HEADS, 128, n), BF),
        pltpu.VMEM((w, n), BF),
        pltpu.VMEM((w, QB), F32),
        pltpu.VMEM((HEADS, QB), F32),
        pltpu.VMEM((HEADS, QB), F32),
    ]


def self_fwd(tab, x, ids, w, wout, ln):
    n, w_ = x.shape
    return call(self_fwd_kernel,
                [((w_, n), BF), ((n, w_), BF), ((n, w_), BF), ((w_, n), BF), ((HEADS, n), F32), ((n, w_), BF), ((n, w_), BF)],
                fwd_scratch(n, w_), 10 << 30, 1, tab, x, ids, w, wout, ln)


def cross_fwd(tab, h, kv, qids, kids, w, ln):
    n, w_ = h.shape
    return call(cross_fwd_kernel,
                [((w_, n), BF), ((w_, n), BF), ((HEADS, n), F32), ((n, w_), BF), ((n, w_), BF)],
                fwd_scratch(n, w_), 10 << 30, 1, tab, h, kv, qids, kids, w, ln)


def bwd_scratch(n, w):
    return [
        pltpu.VMEM((HEADS, n, 128), BF),
        pltpu.VMEM((w, n), BF),
        pltpu.VMEM((HEADS, n, 128), BF),
        pltpu.VMEM((HEADS, 128, n), BF),
        pltpu.VMEM((HEADS, 128, n), BF),
        pltpu.VMEM((w, n), BF),
        pltpu.VMEM((w, QB), F32),
        pltpu.VMEM((3 * w, n), F32),
        pltpu.VMEM((3 * w, n), BF),
    ]


def self_bwd(tab, dh, res, x, ids, qT, k, v, attT, lse, w, wout, ln, dx_type):
    n, w_ = x.shape
    return call(self_bwd_kernel,
                [((n, w_), dx_type), ((3 * w_, w_), BF), ((w_, w_), BF), ((2, w_), F32)],
                bwd_scratch(n, w_) + [pltpu.VMEM((n, w_), BF)], 25 << 30, 1,
                tab, dh, res, x, ids, qT, k, v, attT, lse, w, wout, ln)


def cross_bwd(tab, dr, h, mem, qids, kids, qT, kv, attT, lse, w, wkv):
    n, w_ = h.shape
    return call(cross_bwd_kernel,
                [((n, w_), BF), ((n, w_), BF), ((w_, w_), BF), ((w_, w_), BF), ((2 * w_, w_), BF)],
                bwd_scratch(n, w_), 25 << 30, 1,
                tab, dr, h, mem, qids, kids, qT, kv, attT, lse, w, wkv)


def enc_ffn_fwd(e1, win, b_in, wout, bout, ln, wkv):
    n, w_ = e1.shape
    ff = win.shape[1]
    return call(enc_ffn_fwd_kernel,
                [((n, ff), BF), ((n, ff), BF), ((n, w_), BF), ((n, w_), BF), ((n, 2 * w_), BF)],
                [], 6 << 30, 0, e1, win, b_in, wout, bout, ln, wkv)


def enc_ffn_bwd(dmem, r, g, gp, e1, win, wout, ln):
    n, w_ = e1.shape
    ff = win.shape[1]
    return call(enc_ffn_bwd_kernel,
                [((n, w_), BF), ((w_, ff), BF), ((w_, ff), BF), ((4, w_), F32), ((1, ff), F32), ((1, w_), F32)],
                [pltpu.VMEM((n, ff), BF), pltpu.VMEM((n, w_), BF)], 9 << 30, 0,
                dmem, r, g, gp, e1, win, wout, ln)


def dec_ffn(h, res, cot, win, b_in, wout, bout, ln):
    n, w_ = h.shape
    ff = win.shape[1]
    return call(dec_ffn_kernel,
                [((n, w_), BF), ((n, w_), BF), ((w_, ff), BF), ((w_, ff), BF), ((4, w_), F32), ((1, ff), F32), ((1, w_), F32)],
                [pltpu.VMEM((n, ff), BF), pltpu.VMEM((TB, ff), BF), pltpu.VMEM((n, ff), BF), pltpu.VMEM((n, w_), BF)], 13 << 30, 0,
                h, res, cot, win, b_in, wout, bout, ln)


def block_table(query_ids, key_ids, causal):
    n = query_ids.shape[0]
    starts = jnp.sum((key_ids[None, :] < jnp.arange(5, dtype=jnp.int32)[:, None]).astype(jnp.int32), axis=1)
    first = query_ids[::QB]
    last = query_ids[QB - 1 :: QB]
    lo = starts[first] // CK
    hi = (starts[last + 1] + CK - 1) // CK
    qb = jnp.arange(n // QB, dtype=jnp.int32)
    diag = qb * (QB // CK)
    kd = jnp.where(causal, diag, hi)
    hi = jnp.where(causal, jnp.minimum(hi, diag + QB // CK), hi)
    lo = jnp.minimum(lo, kd)
    return jnp.stack([lo, kd, hi], axis=1)


def row_step(x, y, cot, src, tgt, enc, dec):
    def ln(p, *idx):
        return jnp.stack([p[7 + s][i] for i in idx for s in (0, 1)])
    src_row, tgt_row = src[None, :], tgt[None, :]
    tab_e = block_table(src, src, False)
    tab_d = block_table(tgt, tgt, True)
    tab_c = block_table(tgt, src, False)
    eq, ek, ev, eatt, else_, er, e1 = self_fwd(tab_e, x, src_row, enc[0], enc[1], ln(enc, 0))
    dq, dk, dv, datt, dlse, dr, d1 = self_fwd(tab_d, y, tgt_row, dec[0], dec[1], ln(dec, 0))
    g, gp, r2, mem, kv = enc_ffn_fwd(e1, enc[3], enc[4], enc[5], enc[6], ln(enc, 1, 2), enc[2])
    cq, catt, clse, cr, d2 = cross_fwd(tab_c, d1, kv, tgt_row, src_row, dec[2], ln(dec, 1))
    out, dres, ddwin, ddwoutT, ddln, ddbin, ddbout = dec_ffn(d2, cr, cot, dec[3], dec[4], dec[5], dec[6], ln(dec, 1, 2))
    dh1, dmem, dwqT, dwo, dwkvT = cross_bwd(tab_c, dres, d1, mem, tgt_row, src_row, cq, kv, catt, clse, dec[2], enc[2])
    de1, edwin, edwoutT, edln, edbin, edbout = enc_ffn_bwd(dmem, r2, g, gp, e1, enc[3], enc[5], ln(enc, 1, 2))
    dy, ddqkvT, ddout, ddln1 = self_bwd(tab_d, dh1, dr, y, tgt_row, dq, dk, dv, datt, dlse, dec[0], dec[1], ln(dec, 0), F32)
    dx, edqkvT, edout, edln1 = self_bwd(tab_e, de1, er, x, src_row, eq, ek, ev, eatt, else_, enc[0], enc[1], ln(enc, 0), F32)
    enc_g = (edqkvT, edout, dwkvT, edwin, edwoutT, edln1, edln, edbin, edbout)
    dec_g = (ddqkvT, ddout, jnp.concatenate([dwqT, dwo.T], 0), ddwin, ddwoutT, ddln1, ddln, ddbin, ddbout)
    return mem, out, dx, dy, enc_g, dec_g


def swap(value):
    return lax.ppermute(value, "section", [(0, 1), (1, 0)])


def far_weight(weight):
    n = lax.axis_size("dp")
    index = lax.axis_index("dp")
    rows = weight.shape[0] // n
    part = lax.dynamic_slice_in_dim(weight, index * rows, rows, 0)
    return lax.all_gather(swap(part), "dp", axis=0, tiled=True)


def sum_grads(first, second, sec):
    n = lax.axis_size("dp")
    def flat(parts):
        return jnp.concatenate([p.reshape(n, -1).astype(BF) for p in parts], axis=1)
    both = jnp.stack([flat(first), flat(second)], axis=1)
    mine = lax.psum_scatter(both, "dp", scatter_dimension=0, tiled=True)[0]
    keep = lax.dynamic_index_in_dim(mine, sec, 0, keepdims=False)
    give = lax.dynamic_index_in_dim(mine, 1 - sec, 0, keepdims=False)
    total = keep.astype(F32) + swap(give).astype(F32)
    every = lax.all_gather(total.astype(BF), "dp", axis=0, tiled=False)
    out, at = [], 0
    for p in first:
        size = p.size // n
        out.append(every[:, at : at + size].reshape(p.shape).astype(F32))
        at += size
    return out


def shards(layer_input, cotangent, src_segments, tgt_segments, attn_qkv, attn_out, cross_proj,
           ffn_in, ffn_in_bias, ffn_out, ffn_out_bias, norm_gain, norm_bias):
    sec = lax.axis_index("section")
    first = sec == 0
    own = layer_input[0, :, 0]
    pick = lambda a, i: lax.dynamic_index_in_dim(a, i, 0, keepdims=False)
    keep, away = pick(own, sec), swap(pick(own, 1 - sec))
    x = jnp.where(first, keep, away)
    y = jnp.where(first, away, keep)
    near = [attn_qkv[0], attn_out[0], cross_proj[0], ffn_in[0], ffn_in_bias, ffn_out[0], ffn_out_bias, norm_gain[0], norm_bias[0]]
    far = [far_weight(w) if w.ndim == 2 and w.dtype == BF else swap(w) for w in near]
    enc = [jnp.where(first, a, b) for a, b in zip(near, far)]
    dec = [jnp.where(first, b, a) for a, b in zip(near, far)]
    mem, out, dx, dy, eg, dg = row_step(
        x, y, pick(cotangent[:, 0], sec), pick(src_segments[:, 0], sec), pick(tgt_segments[:, 0], sec), enc, dec)
    there = swap(jnp.where(first, out, mem))
    here = jnp.where(first, mem, out)
    layer_output = jnp.where(first, jnp.stack([here, there]), jnp.stack([there, here]))
    there = swap(jnp.where(first, dy, dx).astype(BF)).astype(F32)
    here = jnp.where(first, dx, dy)
    input_grad = jnp.where(first, jnp.stack([here, there]), jnp.stack([there, here]))
    tot = sum_grads(eg[:5], dg[:5], sec)
    def small(g):
        return jnp.concatenate([g[5], g[6], g[7].reshape(-1, 512), g[8]], axis=0)
    both = lax.psum(jnp.stack([small(eg), small(dg)]), "dp")
    s = pick(both, sec) + swap(pick(both, 1 - sec))
    gain = jnp.stack([s[0], s[2], s[4]])
    shift = jnp.stack([s[1], s[3], s[5]])
    cross = tot[2].T
    return (layer_output[None, :, None], input_grad[None, :, None], tot[0].T[None], tot[1][None], cross[None], tot[3][None],
            s[6:10].reshape(1, -1), tot[4].T[None], s[10:11], gain[None], shift[None])


def solution(mesh):
    return jax.shard_map(
        shards,
        mesh=mesh,
        in_specs=(
            P("section", None, "dp", None, None),
            P(None, "dp", None, None),
            P(None, "dp", None),
            P(None, "dp", None),
            P("section", None, None),
            P("section", None, None),
            P("section", None, None),
            P("section", None, None),
            P("section", None),
            P("section", None, None),
            P("section", None),
            P("section", None, None),
            P("section", None, None),
        ),
        out_specs=(
            P("section", None, "dp", None, None),
            P("section", None, "dp", None, None),
            P("section", None, None),
            P("section", None, None),
            P("section", None, None),
            P("section", None, None),
            P("section", None),
            P("section", None, None),
            P("section", None),
            P("section", None, None),
            P("section", None, None),
        ),
        check_vma=False,
    )
```

time: 1540 us -> 989 us (0.64)
  matrix products: 454 us -> 0 us
  Pallas kernels: 0 us -> 323 us
  starting transfers between devices: 307 us -> 17.7 us
  other arithmetic: 175 us -> 63.2 us
  blocking collectives: 62.1 us -> 83.9 us
  local copies, waits for them, and re-layouts: 152 us -> 131 us
  loops' own time: 18.8 us -> 0 us
    dot_general x72 -> x0, matrix products: 454 us -> none  [the longest x16 131 us: product(): return jnp.dot(left, right, preferred_element_type=jnp.float32)]
    pallas_call x0 -> x9, Pallas kernels: none -> 323 us  [call(): pl.pallas_call(kernel, out_shape=[jax.ShapeDtypeStruct(s, d) for s, d in...]
    ppermute x3 -> x14, starting transfers between devices: 307 us -> 17.2 us  [swap(): return lax.ppermute(value, 'section', [(0, 1), (1, 0)])]
    unnamed x1 -> x7, waiting for transfers between devices: 0.02 us -> 273 us
    psum x1 -> x0, waiting for transfers between devices: 206 us -> none  [shards(): lax.psum((grads[0], grads[1], grads[2], grads[3], grads[4], grads[5], gra...]
    sub x4 -> x3, other arithmetic: 82.4 us -> 0.01 us  [block_table(): hi = (starts[last + 1] + CK - 1) // CK]
    ppermute x3 -> x14, waiting for transfers between devices: 139 us -> 65.3 us  [swap(): return lax.ppermute(value, 'section', [(0, 1), (1, 0)])]
    convert_element_type x4 -> x3, other arithmetic: 42.2 us -> 2.52 us  [the longest x1 1.11 us: sum_grads(): out.append(every[:, at:at + size].reshape(p.shape).astype(F32))]
  transfers between devices with their start and end apart: 4 -> 20, of which waited for: 4 -> 8; matrix products, arithmetic and copies ran while one was open for 0% -> 5% of each run, Pallas kernels for 0% -> 8%
where the time goes in v1:
time: 989 us; the launch traced here: 979 us
  waiting for transfers between devices  344 us (35%)
  Pallas kernels  323 us (33%)
  local copies, waits for them, and re-layouts  131 us (13%)
  blocking collectives  83.9 us (8%)
  other arithmetic  63.2 us (6%)
  starting transfers between devices  17.7 us (2%)
  between operations  15.8 us (2%)
    pallas_call x9, Pallas kernels, call(): pl.pallas_call(kernel, out_shape=[jax.ShapeDtypeStruct(s, d) for s, d in...  323 us
    unnamed x7, waiting for transfers between devices  273 us
    ppermute x14, waiting for transfers between devices, swap(): return lax.ppermute(value, 'section', [(0, 1), (1, 0)])  65.3 us
    psum x1, blocking collectives, shards(): both = lax.psum(jnp.stack([small(eg), small(dg)]), 'dp')  60.6 us
    another operation x1, local copies, waits for them, and re-layouts, sum_grads(): both = jnp.stack([flat(first), flat(second)], axis=1)  36 us
    unnamed x90, local copies, waits for them, and re-layouts  29.5 us
    all_gather x1, blocking collectives, far_weight(): return lax.all_gather(swap(part), 'dp', axis=0, tiled=True)  23.3 us
    reshape x10, local copies, waits for them, and re-layouts, flat(): return jnp.concatenate([p.reshape(n, -1).astype(BF) for p in parts], axis=1)  22.1 us
  transfers between devices with their start and end apart: 20, of which 8 were waited for; matrix products, arithmetic and copies ran while one was open for 5% of the time, Pallas kernels for 8%

profile of v1, /device:TPU:0, one launch (start us, length us, event | category | flops | bytes accessed | tf_op | source)
XLA Modules:
  0.0 978.6 jit_solution(15332236155134478616)
XLA Ops:
  30.3 16.6 %collective-permute-done.5 = bf16[32,2048]{1,0:T(8,128)(2,1)S(1)} collective-permute-done((bf16[32,2048]{1,0:T(8,128)(2,1)S(1)}, bf16[32,2048]{1,0:T(8,128)(2,1)S(1)}, u32[]{:S(2)}, u32[]{:S(2)}) %collective-permute-start.5) | collective-permute-done | bytes 131104 | tf_op jit(solution)/shard_map/ppermute | solution.py:588
  59.8 23.3 %all_gather.22 = bf16[512,512]{1,0:T(8,128)(2,1)S(1)} all-gather(bf16[32,512]{1,0:T(8,128)(2,1)S(1)} %collective-permute-done.2), channel_id=1, replica_groups=mesh['section'=2,'dp'=16] {'dp'}, dimensions={0}, use_global_device_ids=true | all-gather | bytes 557056 | tf_op jit(solution)/shard_map/all_gather | solution.py:596
  90.5 5.3 all-gather.7.cloned.1.call-done
  99.1 42.0 %self_fwd_kernel.2 = (bf16[512,1024]{1,0:T(8,128)(2,1)}, bf16[1024,512]{1,0:T(8,128)(2,1)}, bf16[1024,512]{1,0:T(8,128)(2,1)}, bf16[512,1024]{1,0:T(8,128)(2,1)}...) custom-call(s32[4,3]{1,0:T(4,128)} %pad_add_fusion.tab_ref, ...), custom_call_target="tpu_custom_call" | custom-call | flops 10737418240 | bytes 8388608 | tf_op jit(solution)/shard_map/self_fwd_kernel/pallas_call | solution.py:458
  141.1 36.8 %self_fwd_kernel.3 = (bf16[512,1024]{1,0:T(8,128)(2,1)}, bf16[1024,512]{1,0:T(8,128)(2,1)}, bf16[1024,512]{1,0:T(8,128)(2,1)}, bf16[512,1024]{1,0:T(8,128)(2,1)}...) custom-call(s32[4,3]{1,0:T(4,128)} %pad_add_fusion.2.tab_ref, ...), custom_call_target="tpu_custom_call" | custom-call | flops 10737418240 | bytes 8388608 | tf_op jit(solution)/shard_map/self_fwd_kernel/pallas_call | solution.py:458
  182.1 4.5 bitcast_select_fusion
  186.6 17.7 %enc_ffn_fwd_kernel.1 = (bf16[1024,2048]{1,0:T(8,128)(2,1)}, bf16[1024,2048]{1,0:T(8,128)(2,1)}, bf16[1024,512]{1,0:T(8,128)(2,1)}, bf16[1024,512]{1,0:T(8,128)(2,1)}, bf16[1024,1024]{1,0:T(8,128)(2,1)}) custom-call(bf16[1024,512]{1,0:T(8,128)(2,1)} %get-tuple-element.61.e1_ref, bf16[512,2048]{1,0:T(8,128)(2,1)} %get-tuple-element.166.win_ref, ...), custom_call_target="tpu_custom_call" | custom-call | flops 6442450944 | bytes 8388608 | tf_op jit(solution)/shard_map/enc_ffn_fwd_kernel/pallas_call | solution.py:458
  204.3 40.1 %cross_fwd_kernel.1 = (bf16[512,1024]{1,0:T(8,128)(2,1)}, bf16[512,1024]{1,0:T(8,128)(2,1)}, f32[8,1024]{1,0:T(8,128)}, bf16[1024,512]{1,0:T(8,128)(2,1)}, bf16[1024,512]{1,0:T(8,128)(2,1)}) custom-call(s32[4,3]{1,0:T(4,128)} %pad_add_fusion.1.tab_ref, bf16[1024,512]{1,0:T(8,128)(2,1)} %get-tuple-element.63.h_ref, ...), custom_call_target="tpu_custom_call" | custom-call | flops 10737418240 | bytes 8388608 | tf_op jit(solution)/shard_map/cross_fwd_kernel/pallas_call | solution.py:458
  244.3 27.0 %dec_ffn_kernel.1 = (bf16[1024,512]{1,0:T(8,128)(2,1)}, bf16[1024,512]{1,0:T(8,128)(2,1)}, bf16[512,2048]{1,0:T(8,128)(2,1)}, bf16[512,2048]{1,0:T(8,128)(2,1)},...) custom-call(bf16[1024,512]{1,0:T(8,128)(2,1)} %get-tuple-element.65.h_ref, ...), custom_call_target="tpu_custom_call" | custom-call | flops 13958643712 | bytes 8388608 | tf_op jit(solution)/shard_map/dec_ffn_kernel/pallas_call | solution.py:458
  271.3 45.8 %cross_bwd_kernel.1 = (bf16[1024,512]{1,0:T(8,128)(2,1)}, bf16[1024,512]{1,0:T(8,128)(2,1)}, bf16[512,512]{1,0:T(8,128)(2,1)}, bf16[512,512]{1,0:T(8,128)(2,1)}, bf16[1024,512]{1,0:T(8,128)(2,1)}) custom-call(s32[4,3]{1,0:T(4,128)} %pad_add_fusion.1.tab_ref, bf16[1024,512]{1,0:T(8,128)(2,1)} %get-tuple-element.68.dr_ref, ...), custom_call_target="tpu_custom_call" | custom-call | flops 26843545600 | bytes 8388608 | tf_op jit(solution)/shard_map/cross_bwd_kernel/pallas_call | solution.py:458
  317.1 23.2 %enc_ffn_bwd_kernel.1 = (bf16[1024,512]{1,0:T(8,128)(2,1)}, bf16[512,2048]{1,0:T(8,128)(2,1)}, bf16[512,2048]{1,0:T(8,128)(2,1)}, f32[4,512]{1,0:T(4,128)}, f32[1,2048]{1,0:T(1,128)}, /*index=5*/f32[1,512]{1,0:T(1,128)}) custom-call(bf16[1024,512]{1,0:T(8,128)(2,1)} %get-tuple-element.72.dmem_ref, bf16[1024,512]{1,0:T(8,128)(2,1)} %get-tuple-element.73.r_ref, ...), custom_call_target="tpu_custom_call" | custom-call | flops 9663676416 | bytes 8388608 | tf_op jit(solution)/shard_map/enc_ffn_bwd_kernel/pallas_call | solution.py:458
  340.3 48.1 %self_bwd_kernel.2 = (f32[1024,512]{1,0:T(8,128)}, bf16[1536,512]{1,0:T(8,128)(2,1)}, bf16[512,512]{1,0:T(8,128)(2,1)}, f32[2,512]{1,0:T(2,128)}) custom-call(s32[4,3]{1,0:T(4,128)} %pad_add_fusion.tab_ref, bf16[1024,512]{1,0:T(8,128)(2,1)} %get-tuple-element.76.dh_ref, bf16[1024,512]{1,0:T(8,128)(2,1)} %get-tuple-element.77.res_ref, ...), custom_call_target="tpu_custom_call" | custom-call | flops 26843545600 | bytes 8388608 | tf_op jit(solution)/shard_map/self_bwd_kernel/pallas_call | solution.py:458
  407.3 42.2 %self_bwd_kernel.3 = (f32[1024,512]{1,0:T(8,128)}, bf16[1536,512]{1,0:T(8,128)(2,1)}, bf16[512,512]{1,0:T(8,128)(2,1)}, f32[2,512]{1,0:T(2,128)}) custom-call(s32[4,3]{1,0:T(4,128)} %pad_add_fusion.2.tab_ref, bf16[1024,512]{1,0:T(8,128)(2,1)} %get-tuple-element.84.dh_ref, bf16[1024,512]{1,0:T(8,128)(2,1)} %get-tuple-element.85.res_ref, ...), custom_call_target="tpu_custom_call" | custom-call | flops 26843545600 | bytes 8388608 | tf_op jit(solution)/shard_map/self_bwd_kernel/pallas_call | solution.py:458
  476.2 5.8 pad_maximum_fusion
  482.0 36.0 %copy.163 = bf16[16,2,229376]{2,1,0:T(2,128)(2,1)} copy(bf16[16,2,229376]{2,0,1:T(8,128)(2,1)S(1)} %pad_maximum_fusion) | data formatting | bytes 29360128 | tf_op jit(solution)/shard_map/stack | solution.py:603
  520.0 273.1 %all-reduce.3.cloned.1.call-done = bf16[16,2,229376]{2,1,0:T(2,128)(2,1)} async-done(((bf16[16,2,229376]{2,1,0:T(2,128)(2,1)}), bf16[16,2,229376]{2,1,0:T(2,128)(2,1)}) %all-reduce.3.cloned.1.call-update) | async-done | bytes 14680080
  793.1 9.0 dynamic-slice_reduce_fusion
  803.6 10.6 %collective-permute-done.12 = bf16[229376]{0:T(1024)(128)(2,1)S(1)} collective-permute-done((bf16[229376]{0:T(1024)(128)(2,1)S(1)}, bf16[229376]{0:T(1024)(128)(2,1)S(1)}, u32[]{:S(2)}, u32[]{:S(2)}) %collective-permute-start.12) | collective-permute-done | bytes 458784 | tf_op jit(solution)/shard_map/ppermute | solution.py:588
  817.1 60.6 %psum.7 = f32[2,11,512]{2,1,0:T(8,128)S(1)} all-reduce(f32[2,11,512]{2,1,0:T(8,128)S(1)} %pad_maximum_fusion.2), channel_id=1, replica_groups=mesh['section'=2,'dp'=16] {'dp'}, use_global_device_ids=true, to_apply=%region_3.4 | all-reduce | flops 11264 | bytes 90112 | tf_op jit(solution)/shard_map/psum | solution.py:641
  886.2 20.5 %collective-permute-done.10 = bf16[1024,512]{1,0:T(8,128)(2,1)S(1)} collective-permute-done((bf16[1024,512]{1,0:T(8,128)(2,1)S(1)}, bf16[1024,512]{1,0:T(8,128)(2,1)S(1)}, u32[]{:S(2)}, u32[]{:S(2)}) %collective-permute-start.10) | collective-permute-done | bytes 1048608 | tf_op jit(solution)/shard_map/ppermute | solution.py:588
  908.4 15.3 %collective-permute-done.11 = bf16[1024,512]{1,0:T(8,128)(2,1)S(1)} collective-permute-done((bf16[1024,512]{1,0:T(8,128)(2,1)S(1)}, bf16[1024,512]{1,0:T(8,128)(2,1)S(1)}, u32[]{:S(2)}, u32[]{:S(2)}) %collective-permute-start.11) | collective-permute-done | bytes 1048608 | tf_op jit(solution)/shard_map/ppermute | solution.py:588
  926.6 7.0 reshape.652
  933.5 6.1 slice_convert_fusion
  949.4 5.3 copy.166
  (237 shorter events, 140.9 us)
Async XLA Ops:
  7.2 80.4 %all-gather.13.cloned.1.call-start = ((), (), s32[]{:S(2)}) async-start(), calls=%async_computation.3 | async-start | bytes 1114112 | tf_op jit(solution)/shard_map/all_gather | solution.py:596
  8.3 5.2 collective-permute-start.9
  14.2 81.6 %all-gather.7.cloned.1.call-start = ((), (), s32[]{:S(2)}) async-start(), calls=%async_computation | async-start | bytes 1671168 | tf_op jit(solution)/shard_map/all_gather | solution.py:596
  15.1 6.4 collective-permute-start.1
  19.4 65.5 %collective-permute-start = (bf16[1024,512]{1,0:T(8,128)(2,1)}, bf16[1024,512]{1,0:T(8,128)(2,1)}, u32[]{:S(2)}, u32[]{:S(2)}) collective-permute-start(bf16[1024,512]{1,0:T(8,128)(2,1)} %dynamic-slice_bitcast_fusion.1), channel_id=1, source_target_pairs={{0,16},{16,0},{1,17},{17,1},{2,18},{18,2},{3,19},{19,3},{4,20},{20... | collective-permute-start | bytes 3145736 | tf_op jit(solution)/shard_map/ppermute | solution.py:588
  19.4 35.5 %collective-permute-start.3 = (f32[3,512]{1,0:T(4,128)S(1)}, f32[3,512]{1,0:T(4,128)S(1)}, u32[]{:S(2)}, u32[]{:S(2)}) collective-permute-start(f32[3,512]{1,0:T(4,128)S(1)} %bitcast.110), channel_id=1, source_target_pairs={{0,16},{16,0},{1,17},{17,1},{2,18},{18,2},{3,19},{19,3},{4,20},{20... | collective-permute-start | bytes 18440 | tf_op jit(solution)/shard_map/ppermute | solution.py:588
  21.4 34.6 %collective-permute-start.4 = (f32[3,512]{1,0:T(4,128)S(1)}, f32[3,512]{1,0:T(4,128)S(1)}, u32[]{:S(2)}, u32[]{:S(2)}) collective-permute-start(f32[3,512]{1,0:T(4,128)S(1)} %bitcast.109), channel_id=1, source_target_pairs={{0,16},{16,0},{1,17},{17,1},{2,18},{18,2},{3,19},{19,3},{4,20},{20... | collective-permute-start | bytes 18440 | tf_op jit(solution)/shard_map/ppermute | solution.py:588
  22.2 155.7 %all-gather.9.cloned.1.call-start = ((), (), s32[]{:S(2)}) async-start(), calls=%async_computation.1 | async-start | bytes 2228224 | tf_op jit(solution)/shard_map/all_gather | solution.py:596
  22.3 37.5 %collective-permute-start.2 = (bf16[32,512]{1,0:T(8,128)(2,1)S(1)}, bf16[32,512]{1,0:T(8,128)(2,1)S(1)}, u32[]{:S(2)}, u32[]{:S(2)}) collective-permute-start(bf16[32,512]{1,0:T(8,128)(2,1)S(1)} %dynamic-slice_bitcast_fusion.7), channel_id=1, source_target_pairs={{0,16},{16,0},{1,17},{17,1},{2,18},{18,2},{3,19},{19,3},{4,20},{20... | collective-permute-start | bytes 98312 | tf_op jit(solution)/shard_map/ppermute | solution.py:588
  25.2 21.7 %collective-permute-start.5 = (bf16[32,2048]{1,0:T(8,128)(2,1)S(1)}, bf16[32,2048]{1,0:T(8,128)(2,1)S(1)}, u32[]{:S(2)}, u32[]{:S(2)}) collective-permute-start(bf16[32,2048]{1,0:T(8,128)(2,1)S(1)} %dynamic-slice_bitcast_fusion.3), channel_id=1, source_target_pairs={{0,16},{16,0},{1,17},{17,1},{2,18},{18,2},{3,19},{19,3},{4,20},{20... | collective-permute-start | bytes 393224 | tf_op jit(solution)/shard_map/ppermute | solution.py:588
  47.0 6.5 collective-permute-start.8
  48.1 134.0 %all-gather.11.cloned.1.call-start = ((), (), s32[]{:S(2)}) async-start(), calls=%async_computation.2 | async-start | bytes 2228224 | tf_op jit(solution)/shard_map/all_gather | solution.py:596
  53.5 30.7 %collective-permute-start.7 = (bf16[128,512]{1,0:T(8,128)(2,1)S(1)}, bf16[128,512]{1,0:T(8,128)(2,1)S(1)}, u32[]{:S(2)}, u32[]{:S(2)}) collective-permute-start(bf16[128,512]{1,0:T(8,128)(2,1)S(1)} %dynamic-slice_bitcast_fusion.2), channel_id=1, source_target_pairs={{0,16},{16,0},{1,17},{17,1},{2,18},{18,2},{3,19},{19,3},{4,20},{20... | collective-permute-start | bytes 393224 | tf_op jit(solution)/shard_map/ppermute | solution.py:588
  54.9 4.2 collective-permute-start.6
  84.8 708.3 %all-reduce.3.cloned.1.call-start = ((), (), s32[]{:S(2)}) async-start(), calls=%async_computation.5 | async-start | bytes 29360128
  518.0 408.5 %all-gather.15.cloned.1.call-start = ((), (), s32[]{:S(2)}) async-start(), calls=%async_computation.4 | async-start | bytes 7798784 | tf_op jit(solution)/shard_map/all_gather | solution.py:608
  519.9 297.1 %copy-start.25 = (f32[4,512]{1,0:T(4,128)S(1)}, f32[4,512]{1,0:T(4,128)}, u32[]{:S(2)}) copy-start(f32[4,512]{1,0:T(4,128)} %get-tuple-element.104) | copy-start | bytes 24580
  520.0 297.1 %copy-start.24 = (f32[4,512]{1,0:T(4,128)S(1)}, f32[4,512]{1,0:T(4,128)}, u32[]{:S(2)}) copy-start(f32[4,512]{1,0:T(4,128)} %get-tuple-element.108) | copy-start | bytes 24580
  520.0 297.1 %copy-start.32 = (f32[2,512]{1,0:T(2,128)S(1)}, f32[2,512]{1,0:T(2,128)}, u32[]{:S(2)}) copy-start(f32[2,512]{1,0:T(2,128)} %get-tuple-element.107) | copy-start | bytes 12292
  520.0 297.1 %copy-start.33 = (f32[1,512]{1,0:T(1,128)S(1)}, f32[1,512]{1,0:T(1,128)}, u32[]{:S(2)}) copy-start(f32[1,512]{1,0:T(1,128)} %get-tuple-element.110) | copy-start | bytes 6148
  802.1 12.1 %collective-permute-start.12 = (bf16[229376]{0:T(1024)(128)(2,1)S(1)}, bf16[229376]{0:T(1024)(128)(2,1)S(1)}, u32[]{:S(2)}, u32[]{:S(2)}) collective-permute-start(bf16[229376]{0:T(1024)(128)(2,1)S(1)} %get-tuple-element.159), channel_id=1, source_target_pairs={{0,16},{16,0},{1,17},{17,1},{2,18},{18,2},{3,19},{19,3},{4,20},{20... | collective-permute-start | bytes 1376264 | tf_op jit(solution)/shard_map/ppermute | solution.py:588
  877.7 6.1 collective-permute-start.13
  880.6 26.2 %collective-permute-start.10 = (bf16[1024,512]{1,0:T(8,128)(2,1)S(1)}, bf16[1024,512]{1,0:T(8,128)(2,1)S(1)}, u32[]{:S(2)}, u32[]{:S(2)}) collective-permute-start(bf16[1024,512]{1,0:T(8,128)(2,1)S(1)} %get-tuple-element.172), channel_id=1, source_target_pairs={{0,16},{16,0},{1,17},{17,1},{2,18},{18,2},{3,19},{19,3},{4,20},{20... | collective-permute-start | bytes 3145736 | tf_op jit(solution)/shard_map/ppermute | solution.py:588
  882.7 41.0 %collective-permute-start.11 = (bf16[1024,512]{1,0:T(8,128)(2,1)S(1)}, bf16[1024,512]{1,0:T(8,128)(2,1)S(1)}, u32[]{:S(2)}, u32[]{:S(2)}) collective-permute-start(bf16[1024,512]{1,0:T(8,128)(2,1)S(1)} %select_convert_fusion), channel_id=1, source_target_pairs={{0,16},{16,0},{1,17},{17,1},{2,18},{18,2},{3,19},{19,3},{4,20},{20... | collective-permute-start | bytes 3145736 | tf_op jit(solution)/shard_map/ppermute | solution.py:588
  (33 other events, 1553.0 us)
Sparse Core Ops, SparseCore 0:
  14.3 39.7 all-gather.12
  56.9 38.8 all-gather.6
  98.5 40.3 all-gather.8
  141.5 40.5 all-gather.10
  518.2 274.8 all-reduce.2
  815.2 68.8 all-gather.14
